TPU v7x, 32 devices: a whole 2x2x4 slice. The times are simulated.
32 devices in a mesh: node: 8 (over z, y), ctr: 4 (over x, core).
Axes of the slice: x: 2, y: 2, z: 4, core: 2. Of those that a mesh axis runs over, the one named last changes fastest.
Arguments:
- surface_xyz: float32 [3, 65536], P(None, ('node', 'ctr')), may hold values from 0 to 1
- centre_idx: int32 [32768], P(('node', 'ctr')), may hold values from 0 to 65535, as said below
- volume_xyz: float32 [3, 32768], P(None, 'node'), may hold values from 0 to 1
- slab_ids: int32 [32768], P('node'), may hold values from 0 to 32767, as said below
- cotangent: float32 [12, 32768], P(None, 'node'), may hold values from -6 to 6
Outputs:
- coef_adjoint: float32 [12, 32768], P(None, ('node', 'ctr'))
- residual: float32 [12, 32768], P(None, ('node', 'ctr'))
Inputs may be any that keep to these rules, and one draw needn't show every extreme that they name: `centre_idx`: all entries are distinct, and 0 and 65535 are always among them. `slab_ids`: within each aligned block of 4096 entries (the nodes of one index of node) the entries are the ids of that same block, each once.
All inputs are finite; a program needn't handle non-finite values.
Results may differ from a plain program's by a relative error of at most 0.0003.
Values sent between devices are 32-bit elements; how exact they have to be, the bound alone decides.
A program may use at most 320 MiB of HBM per device.

v0:
```python
import functools
import math

import jax
import jax.numpy as jnp
from jax import lax
from jax.experimental import pallas as pl
from jax.experimental.pallas import tpu as pltpu
from jax.sharding import PartitionSpec as P

RADIUS = 0.2
LANES = 128
PAD = 16
LIFT = 2.0**17
VMEM = 50 * 1024 * 1024
NT = (((1,), (1,)), ((), ()))


def split3(value):
    first = lax.reduce_precision(value, 8, 7)
    rest = value - first
    second = lax.reduce_precision(rest, 8, 7)
    return first, second, lax.reduce_precision(rest - second, 8, 7)


def lookup(table, ids):
    rows = table.shape[1] // LANES
    parts = jnp.concatenate([part.reshape(3, rows, LANES) for part in split3(table)], axis=0)
    parts = parts.transpose(1, 0, 2).reshape(rows, 9 * LANES).astype(jnp.bfloat16)
    high = (ids[:, None] // LANES == jnp.arange(rows, dtype=jnp.int32)[None, :]).astype(jnp.bfloat16)
    picked = jnp.dot(high, parts, preferred_element_type=jnp.float32)
    low = ids[:, None] % LANES == jnp.arange(LANES, dtype=jnp.int32)[None, :]
    picked = picked.reshape(-1, 9, LANES)
    picked = jnp.sum(jnp.where(low[:, None, :], picked, 0.0), axis=2)
    return (picked[:, 0:3] + picked[:, 3:6] + picked[:, 6:9]).T


def scaled(xyz):
    point = (xyz - 0.5) * (1.0 / RADIUS)
    return jnp.concatenate([point, jnp.ones((1, xyz.shape[1]), jnp.float32)], axis=0)


def row_features(point):
    square = jnp.sum(point[:3] * point[:3], axis=0, keepdims=True)
    alpha = jnp.concatenate(
        [jnp.ones_like(square), jnp.zeros_like(point[:3]), -2.0 * point[:3], square], axis=0
    )
    a1, a2, a3 = split3(alpha)
    return jnp.concatenate([a1, a1, a2, a2, a1, a3], axis=0).T.astype(jnp.bfloat16)


def rounded(value):
    return value.astype(jnp.bfloat16).astype(jnp.float32)


def right_factor(group):
    row = lax.broadcasted_iota(jnp.int32, group.shape, 0)
    place = jnp.where(row >= 4, group, 0.0)
    square = jnp.sum(jnp.where(row < 7, place * place, 0.0), axis=0, keepdims=True)
    beta = jnp.where(row == 0, square, place)
    b1 = rounded(beta)
    rest = beta - b1
    b2 = rounded(rest)
    b3 = rest - b2
    return jnp.concatenate([b1, b2, b1, b2, b3, b1], axis=0).astype(jnp.bfloat16)


def two_parts(vectors):
    v1 = rounded(vectors)
    return jnp.concatenate([v1, vectors - v1], axis=0).astype(jnp.bfloat16)


def finish(acc, out_ref):
    total = acc[...].T
    out_ref[...] = 4.0 * (total[:PAD] + total[PAD:])


def side_by_side(make, ref):
    return jnp.concatenate([make(ref[index]) for index in range(ref.shape[0])], axis=1)


def apply_body(row_tile, keep, left_ref, beta_ref, vec_ref, out_ref, *rest):
    if keep:
        hi_ref, lo_ref, acc = rest
    else:
        (acc,) = rest
    rows = left_ref.shape[0]
    step = pl.program_id(0)

    @pl.when(step == 0)
    def _():
        acc[...] = jnp.zeros_like(acc)

    right = side_by_side(right_factor, beta_ref)
    vec = side_by_side(two_parts, vec_ref)
    vec = jnp.concatenate([vec, vec], axis=1)

    for index in range(rows // row_tile):
        here = pl.ds(index * row_tile, row_tile)
        q = jnp.dot(left_ref[here, :], right, preferred_element_type=jnp.float32)
        q = jnp.minimum(jnp.maximum(q, 1e-30), 1.0)
        s = q * lax.rsqrt(q)
        w = 1.0 - s
        w2 = w * w
        k = (w2 * w2) * (0.25 + s)
        hi = k.astype(jnp.bfloat16)
        rest_k = k - hi.astype(jnp.float32)
        lo = rest_k.astype(jnp.bfloat16)
        if keep:
            hi_ref[here, :] = hi
            lo_ref[here, :] = (rest_k * LIFT).astype(jnp.float8_e4m3fn)
        acc[here, :] += lax.dot_general(
            jnp.concatenate([hi, lo], axis=1), vec, NT, preferred_element_type=jnp.float32
        )

    @pl.when(step == pl.num_programs(0) - 1)
    def _():
        finish(acc, out_ref)


def stored_body(hi_ref, lo_ref, vec_ref, out_ref, acc):
    step = pl.program_id(0)

    @pl.when(step == 0)
    def _():
        acc[...] = jnp.zeros_like(acc)

    vec = side_by_side(two_parts, vec_ref)
    acc[...] += lax.dot_general(
        hi_ref[...], vec, NT, preferred_element_type=jnp.float32
    ) + lax.dot_general(
        lo_ref[...].astype(jnp.bfloat16), vec * (1.0 / LIFT), NT, preferred_element_type=jnp.float32)

    @pl.when(step == pl.num_programs(0) - 1)
    def _():
        finish(acc, out_ref)


def apply_kernel(left, beta, vec, beta_block, vec_block, beta_map, vec_map, steps, keep):
    rows = left.shape[0]
    block = beta_block[0] * beta_block[2]
    row_tile = math.gcd(rows, 256)
    out_shape = [jax.ShapeDtypeStruct((PAD, rows), jnp.float32)]
    out_specs = [pl.BlockSpec((PAD, rows), lambda j: (0, 0))]
    if keep:
        kept = (rows, steps * block)
        out_shape += [jax.ShapeDtypeStruct(kept, jnp.bfloat16)]
        out_shape += [jax.ShapeDtypeStruct(kept, jnp.float8_e4m3fn)]
        out_specs += [pl.BlockSpec((rows, block), lambda j: (0, j))] * 2
    return pl.pallas_call(
        functools.partial(apply_body, row_tile, keep),
        grid=(steps,),
        in_specs=[
            pl.BlockSpec(left.shape, lambda j: (0, 0)),
            pl.BlockSpec(beta_block, beta_map),
            pl.BlockSpec(vec_block, vec_map),
        ],
        out_shape=out_shape,
        out_specs=out_specs,
        scratch_shapes=[pltpu.VMEM((rows, 2 * PAD), jnp.float32)],
        compiler_params=pltpu.CompilerParams(vmem_limit_bytes=VMEM),
        cost_estimate=pl.CostEstimate(
            flops=rows * steps * block * 3000, bytes_accessed=1 << 20, transcendentals=0
        ),
    )(left, beta, vec)


def apply_stored(hi, lo, vec):
    rows = hi.shape[0]
    chunks, _, chunk = vec.shape
    group = math.gcd(chunks, max(1, 1024 // chunk))
    block = group * chunk
    return pl.pallas_call(
        stored_body,
        grid=(chunks // group,),
        in_specs=[
            pl.BlockSpec((rows, block), lambda j: (0, j)),
            pl.BlockSpec((rows, block), lambda j: (0, j)),
            pl.BlockSpec((group, PAD, chunk), lambda j: (j, 0, 0)),
        ],
        out_shape=jax.ShapeDtypeStruct((PAD, rows), jnp.float32),
        out_specs=pl.BlockSpec((PAD, rows), lambda j: (0, 0)),
        scratch_shapes=[pltpu.VMEM((rows, 2 * PAD), jnp.float32)],
        compiler_params=pltpu.CompilerParams(vmem_limit_bytes=VMEM),
        cost_estimate=pl.CostEstimate(
            flops=rows * chunks * chunk * 128, bytes_accessed=hi.size * 4, transcendentals=0
        ),
    )(hi, lo, vec)


def local(surface_xyz, centre_idx, volume_xyz, slab_ids, cotangent):
    everyone = ("node", "ctr")
    width = cotangent.shape[0]
    surface = lax.all_gather(surface_xyz.reshape(-1), everyone, axis=0)
    devices = surface.shape[0]
    surface = surface.reshape(devices, 3, -1).transpose(1, 0, 2).reshape(3, -1)

    nodes = lookup(volume_xyz, slab_ids % volume_xyz.shape[1])
    packed = jnp.concatenate([cotangent, scaled(nodes)], axis=0)
    packed = lax.all_gather(packed, "node", axis=0)

    mine = scaled(lookup(surface, centre_idx))
    left = row_features(mine)
    beta = lax.all_gather(jnp.concatenate([jnp.zeros_like(mine), mine], axis=0), everyone, axis=0)
    owned = mine.shape[1]
    half = owned // 2

    block = math.gcd(packed.shape[2], 1024)
    per = packed.shape[2] // block
    group = math.gcd(devices, max(1, 1024 // half))
    pulled_parts, gathered = [], []
    for part in range(2):
        pulled = apply_kernel(
            left[part * half : (part + 1) * half],
            packed,
            packed,
            (1, 8, block),
            (1, PAD, block),
            lambda j: (j // per, 1, j % per),
            lambda j: (j // per, 0, j % per),
            per * packed.shape[0],
            False,
        )[0]
        pulled_parts.append(pulled)
        gathered.append(lax.all_gather(pulled, everyone, axis=0))
    pulled = jnp.concatenate(pulled_parts, axis=1)
    pulled_all = jnp.concatenate(gathered, axis=2)

    image = 0.0
    kept = []
    for part in range(2):
        term, hi, lo = apply_kernel(
            left,
            beta,
            gathered[part],
            (group, 8, half),
            (group, PAD, half),
            lambda j, part=part: (j, 0, part),
            lambda j: (j, 0, 0),
            devices // group,
            True,
        )
        image = image + term
        kept.append((hi, lo))
    image_all = lax.all_gather(image, everyone, axis=0)

    real = jnp.arange(PAD) < width

    def safe(value):
        return jnp.where(real, value, 1.0)

    norm = safe(jnp.sum(pulled_all * pulled_all, axis=(0, 2)))
    step_len = norm / safe(jnp.sum(pulled_all * image_all, axis=(0, 2)))
    resid_all = pulled_all - step_len[:, None] * image_all
    norm_next = jnp.sum(resid_all * resid_all, axis=(0, 2))
    ratio = norm_next / norm
    direction_all = resid_all + ratio[:, None] * pulled_all
    solution_mine = step_len[:, None] * pulled
    resid = pulled - step_len[:, None] * image
    direction = resid + ratio[:, None] * pulled

    image = apply_stored(*kept[0], direction_all[:, :, :half]) + apply_stored(
        *kept[1], direction_all[:, :, half:]
    )
    curve = lax.psum(jnp.sum(direction * image, axis=1), everyone)
    step_len = (norm_next / safe(curve))[:, None]
    solution_mine = solution_mine + step_len * direction
    resid = resid - step_len * image
    return (solution_mine[:width], resid[:width])


def solution(mesh):
    return jax.shard_map(
        local,
        mesh=mesh,
        in_specs=(
            P(None, ("node", "ctr")),
            P(("node", "ctr")),
            P(None, "node"),
            P("node"),
            P(None, "node"),
        ),
        out_specs=(P(None, ("node", "ctr")), P(None, ("node", "ctr"))),
        check_vma=False,
    )
```

profile of v0, /device:TPU:0, one launch (start us, length us, event | category | flops | bytes accessed | tf_op | source)
XLA Modules:
  0.0 445.7 jit_solution(8226818803063843644)
XLA Ops:
  8.0 0.9 fusion.21
  9.2 3.0 select_reduce_fusion
  12.4 0.8 maximum_maximum_fusion
  13.3 47.9 %all-gather.5 = f32[32,1,6144]{2,1,0:T(1,128)S(1)} all-gather(f32[1,1,6144]{2,1,0:T(1,128)S(1)} %reshape.167), channel_id=1, replica_groups=mesh['node'=8,'ctr'=4] {'node','ctr'}, dimensions={0}, use_global_device_ids=true | all-gather | bytes 811008 | tf_op jit(solution)/shard_map/all_gather | solution.py:194
  61.3 1.9 reduce
  65.4 1.7 select_reduce_fusion.1
  68.7 1.6 copy-done.4
  70.3 47.6 %shard_map.69 = f32[16,512]{1,0:T(8,128)} custom-call(bf16[512,48]{1,0:T(8,128)(2,1)S(1)} %get-tuple-element.27.left_ref, f32[8,16,4096]{2,1,0:T(8,128)S(1)} %bitcast.66, f32[8,16,4096]{2,1,0:T(8,128)S(1)} %bitcast.67), custom_call_target="tpu_custom_call" | custom-call | flops 50331648000 | bytes 1048576 | tf_op jit(solution)/shard_map/pallas_call | solution.py:150
  118.0 1.6 copy-done.5
  119.6 47.6 %shard_map.68 = f32[16,512]{1,0:T(8,128)} custom-call(bf16[512,48]{1,0:T(8,128)(2,1)S(1)} %get-tuple-element.28.left_ref, f32[8,16,4096]{2,1,0:T(8,128)S(1)} %bitcast.68, f32[8,16,4096]{2,1,0:T(8,128)S(1)} %bitcast.69), custom_call_target="tpu_custom_call" | custom-call | flops 50331648000 | bytes 1048576 | tf_op jit(solution)/shard_map/pallas_call | solution.py:150
  167.4 10.7 %all-gather.16.cloned.1.call-done = f32[512,512]{1,0:T(8,128)} async-done(((f32[16,512]{1,0:T(8,128)}), f32[512,512]{1,0:T(8,128)}) %all-gather.16.cloned.1.call-update) | async-done | bytes 1048592 | tf_op jit(solution)/shard_map/all_gather | solution.py:225
  178.2 1.2 copy-done
  179.4 1.2 copy-done.6
  180.6 49.3 %shard_map.71 = (f32[16,1024]{1,0:T(8,128)S(1)}, bf16[1024,16384]{1,0:T(8,128)(2,1)}, f8e4m3fn[1024,16384]{1,0:T(32,128)(4,1)}) custom-call(bf16[1024,48]{1,0:T(8,128)(2,1)S(1)} %bitcast.64, f32[32,8,1024]{2,1,0:T(8,128)S(1)} %bitcast.70, f32[32,16,512]{2,1,0:T(8,128)S(1)} %bitcast.55), custom_call_target="tpu_custom_call" | custom-call | flops 50331648000 | bytes 1048576 | tf_op jit(solution)/shard_map/pallas_call | solution.py:150
  229.9 3.7 all-gather.14.cloned.1.call-done
  233.5 1.2 copy-done.2
  234.8 49.2 %shard_map.70 = (f32[16,1024]{1,0:T(8,128)S(1)}, bf16[1024,16384]{1,0:T(8,128)(2,1)}, f8e4m3fn[1024,16384]{1,0:T(32,128)(4,1)}) custom-call(bf16[1024,48]{1,0:T(8,128)(2,1)S(1)} %bitcast.65, f32[32,8,1024]{2,1,0:T(8,128)S(1)} %bitcast.71, f32[32,16,512]{2,1,0:T(8,128)S(1)} %bitcast.59), custom_call_target="tpu_custom_call" | custom-call | flops 50331648000 | bytes 1048576 | tf_op jit(solution)/shard_map/pallas_call | solution.py:150
  284.7 55.6 %all-gather.20.cloned.1.call-done = f32[512,1024]{1,0:T(8,128)} async-done(((f32[16,1024]{1,0:T(8,128)}), f32[512,1024]{1,0:T(8,128)}) %all-gather.20.cloned.1.call-update) | async-done | bytes 2097168 | tf_op jit(solution)/shard_map/all_gather | solution.py:245
  340.3 2.1 multiply_reduce_fusion.2
  344.1 27.0 %shard_map.72 = f32[16,1024]{1,0:T(8,128)S(1)} custom-call(bf16[1024,16384]{1,0:T(8,128)(2,1)} %get-tuple-element.10.hi_ref, f8e4m3fn[1024,16384]{1,0:T(32,128)(4,1)} %get-tuple-element.11.lo_ref, f32[32,16,512]{2,1,0:T(8,128)S(1)} %get-tuple-element.23.vec_ref), custom_call_target="tpu_custom_call" | custom-call | flops 2147483648 | bytes 67108864 | tf_op jit(solution)/shard_map/pallas_call | solution.py:173
  371.1 27.1 %shard_map.73 = f32[16,1024]{1,0:T(8,128)S(1)} custom-call(bf16[1024,16384]{1,0:T(8,128)(2,1)} %get-tuple-element.12.hi_ref, f8e4m3fn[1024,16384]{1,0:T(32,128)(4,1)} %get-tuple-element.13.lo_ref, f32[32,16,512]{2,1,0:T(8,128)S(1)} %get-tuple-element.22.vec_ref), custom_call_target="tpu_custom_call" | custom-call | flops 2147483648 | bytes 67108864 | tf_op jit(solution)/shard_map/pallas_call | solution.py:173
  398.2 1.0 multiply_reduce_fusion.3
  399.2 38.5 %psum.7 = f32[16]{0:T(128)S(1)} all-reduce(f32[16]{0:T(128)S(1)} %get-tuple-element.16), channel_id=1, replica_groups=mesh['node'=8,'ctr'=4] {'node','ctr'}, use_global_device_ids=true, to_apply=%region_7.8 | all-reduce | flops 16 | bytes 128 | tf_op jit(solution)/shard_map/psum | solution.py:265
  437.7 1.5 slice_subtract_fusion
  (71 shorter events, 7.8 us)
Async XLA Ops:
  7.2 61.5 %all-gather.12.cloned.1.call-start = ((), (), s32[]{:S(2)}) async-start(), calls=%async_computation | async-start | bytes 2359296 | tf_op jit(solution)/shard_map/all_gather | solution.py:200
  9.2 3.2 copy-start.10
  9.2 4.1 copy-start.11
  13.2 154.2 %all-gather.18.cloned.1.call-start = ((), (), s32[]{:S(2)}) async-start(), calls=%async_computation.3 | async-start | bytes 1081344 | tf_op jit(solution)/shard_map/all_gather | solution.py:204
  64.5 0.8 copy-start.12
  67.8 110.3 %all-gather.16.cloned.1.call-start = ((), (), s32[]{:S(2)}) async-start(), calls=%async_computation.2 | async-start | bytes 1081344 | tf_op jit(solution)/shard_map/all_gather | solution.py:225
  68.7 1.6 copy-start.4
  117.9 115.6 %all-gather.14.cloned.1.call-start = ((), (), s32[]{:S(2)}) async-start(), calls=%async_computation.1 | async-start | bytes 1081344 | tf_op jit(solution)/shard_map/all_gather | solution.py:225
  118.0 1.6 copy-start.5
  167.2 173.1 %all-gather.20.cloned.1.call-start = ((), (), s32[]{:S(2)}) async-start(), calls=%async_computation.4 | async-start | bytes 2162688 | tf_op jit(solution)/shard_map/all_gather | solution.py:245
  178.2 1.2 copy-start
  179.4 1.2 copy-start.6
  180.6 52.9 %copy-start.7 = (f32[256,1024]{1,0:T(8,128)S(1)}, f32[256,1024]{1,0:T(8,128)}, u32[]{:S(2)}) copy-start(f32[256,1024]{1,0:T(8,128)} %all-gather.18.cloned.1.call-done) | copy-start | bytes 3145732
  233.5 1.2 copy-start.2
  234.8 105.5 %copy-start.1 = (f32[512,512]{1,0:T(8,128)S(1)}, f32[512,512]{1,0:T(8,128)}, u32[]{:S(2)}) copy-start(f32[512,512]{1,0:T(8,128)} %all-gather.16.cloned.1.call-done) | copy-start | bytes 3145732
  234.8 105.5 %copy-start.3 = (f32[512,512]{1,0:T(8,128)S(1)}, f32[512,512]{1,0:T(8,128)}, u32[]{:S(2)}) copy-start(f32[512,512]{1,0:T(8,128)} %all-gather.14.cloned.1.call-done) | copy-start | bytes 3145732
  340.3 2.2 copy-start.8
  371.1 27.1 %copy-start.9 = (f32[16,1024]{1,0:T(8,128)S(1)}, f32[16,1024]{1,0:T(8,128)}, u32[]{:S(2)}) copy-start(f32[16,1024]{1,0:T(8,128)} %add.64) | copy-start | bytes 196612
Sparse Core Ops, SparseCore 0:
  13.3 53.6 all-gather.11
  70.5 52.0 all-gather.17
  125.5 52.6 all-gather.15
  180.9 52.6 all-gather.13
  284.8 55.4 all-gather.19
where the time goes:
time: 446 us
  Pallas kernels  248 us (56%)
  blocking collectives  86.5 us (19%)
  waiting for transfers between devices  70.1 us (16%)
  between operations  14.1 us (3%)
  other arithmetic  12.9 us (3%)
  local copies, waits for them, and re-layouts  9.35 us (2%)
  matrix products  4.7 us (1%)
    pallas_call x4, Pallas kernels, apply_kernel(): pl.pallas_call(functools.partial(apply_body, row_tile, keep), grid=(steps...  194 us
    all_gather x1, waiting for transfers between devices, local(): image_all = lax.all_gather(image, everyone, axis=0)  55.6 us
    pallas_call x2, Pallas kernels, apply_stored(): pl.pallas_call(stored_body, grid=(chunks // group,), in_specs=[pl.BlockSp...  54.1 us
    all_gather x1, blocking collectives, local(): surface = lax.all_gather(surface_xyz.reshape(-1), everyone, axis=0)  47.9 us
    psum x1, blocking collectives, local(): curve = lax.psum(jnp.sum(direction * image, axis=1), everyone)  38.5 us
    all_gather x2, waiting for transfers between devices, local(): gathered.append(lax.all_gather(pulled, everyone, axis=0))  14.4 us
  transfers between devices with their start and end apart: 5, of which 3 were waited for; matrix products, arithmetic and copies ran while one was open for 2% of the time, Pallas kernels for 32%

commit v1 on v0

v1 whole, which is shorter than its diff:
```python
import functools
import math

import jax
import jax.numpy as jnp
from jax import lax
from jax.experimental import pallas as pl
from jax.experimental.pallas import tpu as pltpu
from jax.sharding import PartitionSpec as P

RADIUS = 0.2
LANES = 128
GROUP = 32
BATCH = 8
PAIR = 2
CELLS = 5
DEPTH = 64
PAD = 16
VMEM = 50 * 1024 * 1024
NT = (((1,), (1,)), ((), ()))
MESH = pl.DeviceIdType.MESH


def split3(value):
    first = lax.reduce_precision(value, 8, 7)
    rest = value - first
    second = lax.reduce_precision(rest, 8, 7)
    return first, second, lax.reduce_precision(rest - second, 8, 7)


def lookup(table, ids):
    rows = table.shape[1] // LANES
    parts = jnp.concatenate([part.reshape(3, rows, LANES) for part in split3(table)], axis=0)
    parts = parts.transpose(1, 0, 2).reshape(rows, 9 * LANES).astype(jnp.bfloat16)
    high = (ids[:, None] // LANES == jnp.arange(rows, dtype=jnp.int32)[None, :]).astype(jnp.bfloat16)
    picked = jnp.dot(high, parts, preferred_element_type=jnp.float32)
    low = ids[:, None] % LANES == jnp.arange(LANES, dtype=jnp.int32)[None, :]
    picked = picked.reshape(-1, 9, LANES)
    picked = jnp.sum(jnp.where(low[:, None, :], picked, 0.0), axis=2)
    return (picked[:, 0:3] + picked[:, 3:6] + picked[:, 6:9]).T


def scaled(xyz):
    point = (xyz - 0.5) * (1.0 / RADIUS)
    return jnp.concatenate([point, jnp.ones((1, xyz.shape[1]), jnp.float32)], axis=0)


def row_features(point):
    square = jnp.sum(point[:3] * point[:3], axis=0, keepdims=True)
    alpha = jnp.concatenate(
        [jnp.ones_like(square), jnp.zeros_like(point[:3]), -2.0 * point[:3], square], axis=0
    )
    a1, a2, a3 = split3(alpha)
    return jnp.concatenate([a1, a1, a2, a2, a1, a3], axis=0).T.astype(jnp.bfloat16)


def rounded(value):
    return value.astype(jnp.bfloat16).astype(jnp.float32)


def right_factor(group):
    row = lax.broadcasted_iota(jnp.int32, group.shape, 0)
    place = jnp.where(row >= 4, group, 0.0)
    square = jnp.sum(jnp.where(row < 7, place * place, 0.0), axis=0, keepdims=True)
    beta = jnp.where(row == 0, square, place)
    b1 = rounded(beta)
    rest = beta - b1
    b2 = rounded(rest)
    b3 = rest - b2
    return jnp.concatenate([b1, b2, b1, b2, b3, b1], axis=0).astype(jnp.bfloat16)


def two_parts(vectors):
    v1 = rounded(vectors)
    return jnp.concatenate([v1, vectors - v1], axis=0).astype(jnp.bfloat16)


def sort_key(xyz):
    count = xyz.shape[1]
    cell = jnp.minimum((xyz[:2] * CELLS).astype(jnp.int32), CELLS - 1)
    deep = jnp.minimum((xyz[2] * DEPTH).astype(jnp.int32), DEPTH - 1)
    column = cell[0] * CELLS + jnp.where(cell[0] % 2 == 1, CELLS - 1 - cell[1], cell[1])
    deep = jnp.where(column % 2 == 1, DEPTH - 1 - deep, deep)
    return (column * DEPTH + deep) * count + jnp.arange(count, dtype=jnp.int32)


def boxes(points, size):
    tiles = points[:3].reshape(3, -1, size)
    return jnp.min(tiles, axis=2), jnp.max(tiles, axis=2)


def near_lists(tiles, groups):
    gap = jnp.maximum(
        jnp.maximum(tiles[0][:, :, None] - groups[1][:, None, :], groups[0][:, None, :] - tiles[1][:, :, None]),
        0.0,
    )
    near = jnp.sum(gap * gap, axis=0) < 1.0 + 1e-4
    count = jnp.sum(near.astype(jnp.int32), axis=1)
    size = near.shape[1]
    upto = (jnp.arange(size)[:, None] <= jnp.arange(size)[None, :]).astype(jnp.bfloat16)
    seen = jnp.dot(near.astype(jnp.bfloat16), upto, preferred_element_type=jnp.float32).astype(jnp.int32)
    every = jnp.arange(size, dtype=jnp.int32)
    place = jnp.where(near, seen - 1, count[:, None] + every[None, :] - seen)
    order = jnp.sum(
        jnp.where(place[:, :, None] == every[None, None, :], every[None, :, None], 0), axis=1
    )
    return count, order


def apply_body(count, order, left_ref, beta_ref, vec_ref, out_ref, acc, right, vec, items, q0, q1, k0, k1):
    rows = left_ref.shape[0]
    tiles = beta_ref.shape[0]
    span = GROUP * BATCH
    acc[...] = jnp.zeros_like(acc)
    for ref in (q0, q1, k0, k1):
        ref[...] = jnp.zeros_like(ref)

    def prepare(tile, _):
        right[tile] = right_factor(beta_ref[tile])
        parts = two_parts(vec_ref[tile])
        vec[tile] = jnp.concatenate([parts, parts], axis=1)
        return 0

    lax.fori_loop(0, tiles, prepare, 0)
    right[tiles] = jnp.zeros_like(right[tiles])
    vec[tiles] = jnp.zeros_like(vec[tiles])

    nothing = tiles * rows
    for index in range(2 * PAIR):
        items[index] = nothing

    def fill(tile, at):
        def one(batch, at):
            items[at] = tile * rows + batch * BATCH
            return at + 1

        return lax.fori_loop(0, (count[tile] + BATCH - 1) // BATCH, one, at)

    end = lax.fori_loop(0, tiles, fill, 2 * PAIR)
    for index in range(4 * PAIR):
        items[end + index] = nothing

    def item(index):
        code = items[index]
        tile = code // rows
        first = code - tile * rows
        listed = jnp.minimum(tile, tiles - 1)
        return tile, [pl.multiple_of(order[listed, first + i] * GROUP, GROUP) for i in range(BATCH)]

    def step(index, q_in, q_out, k_in, k_out):
        for unit in range(PAIR):
            tile, places = item(index * PAIR + unit)
            part = lax.dot_general(
                k_in[pl.ds(unit * span, span), :], vec[tile], NT, preferred_element_type=jnp.float32
            )
            for j, place in enumerate(places):
                acc[pl.ds(place, GROUP), :] += part[j * GROUP : (j + 1) * GROUP]
        q = jnp.minimum(jnp.maximum(q_in[...], 1e-30), 1.0)
        s = q * lax.rsqrt(q)
        w = 1.0 - s
        w2 = w * w
        k = (w2 * w2) * (0.25 + s)
        hi = k.astype(jnp.bfloat16)
        k_out[:, :LANES] = hi
        k_out[:, LANES:] = (k - hi.astype(jnp.float32)).astype(jnp.bfloat16)
        for unit in range(PAIR):
            tile, places = item((index + 2) * PAIR + unit)
            left = jnp.concatenate([left_ref[pl.ds(place, GROUP), :] for place in places], axis=0)
            q_out[pl.ds(unit * span, span), :] = jnp.dot(
                left, right[tile], preferred_element_type=jnp.float32
            )

    def two_steps(index, _):
        step(2 * index, q0, q1, k0, k1)
        step(2 * index + 1, q1, q0, k1, k0)
        return 0

    steps = (end - 2 * PAIR + PAIR - 1) // PAIR + 2
    lax.fori_loop(0, (steps + 1) // 2, two_steps, 0)

    owners, width, owned = out_ref.shape
    for owner in range(owners):
        total = acc[pl.ds(owner * owned, owned), :].T
        out_ref[owner] = 4.0 * (total[:width] + total[PAD : PAD + width])


def apply_kernel(lists, left, beta, vec, owners):
    count, order = lists
    rows = left.shape[0]
    tiles = beta.shape[0]
    width = vec.shape[1]
    vec = jnp.pad(vec, ((0, 0), (0, PAD - width), (0, 0)))
    wide = PAIR * GROUP * BATCH
    return pl.pallas_call(
        apply_body,
        out_shape=jax.ShapeDtypeStruct((owners, width, rows // owners), jnp.float32),
        in_specs=[pl.BlockSpec(memory_space=pltpu.SMEM)] * 2 + [pl.BlockSpec(memory_space=pltpu.VMEM)] * 3,
        out_specs=pl.BlockSpec(memory_space=pltpu.VMEM),
        scratch_shapes=[
            pltpu.VMEM((rows, 2 * PAD), jnp.float32),
            pltpu.VMEM((tiles + 1, 48, LANES), jnp.bfloat16),
            pltpu.VMEM((tiles + 1, 2 * PAD, 2 * LANES), jnp.bfloat16),
            pltpu.SMEM((tiles * (rows // (GROUP * BATCH)) + 8 * PAIR,), jnp.int32),
            pltpu.VMEM((wide, LANES), jnp.float32),
            pltpu.VMEM((wide, LANES), jnp.float32),
            pltpu.VMEM((wide, 2 * LANES), jnp.bfloat16),
            pltpu.VMEM((wide, 2 * LANES), jnp.bfloat16),
        ],
        compiler_params=pltpu.CompilerParams(vmem_limit_bytes=VMEM),
    )(count, order, left, beta, vec)


def node_rows_body(slab_ref, perm_ref, xyz_ref, cot_ref, xyz_out, cot_out, rows_a, rows_b, rows_c):
    count = cot_ref.shape[1]
    width = cot_ref.shape[0]
    blank = jnp.zeros((PAD - width, LANES), jnp.float32)
    for tile in range(count // LANES):
        here = pl.ds(tile * LANES, LANES)
        rows_a[here, :PAD] = jnp.concatenate([cot_ref[:, here], blank], axis=0).T

    def scatter(index, _):
        base = pl.multiple_of(index * 16, 16)
        for i in range(16):
            rows_b[pl.ds(slab_ref[base + i], 1), :] = rows_a[pl.ds(base + i, 1), :]
        return 0

    lax.fori_loop(0, count // 16, scatter, 0)
    for tile in range(count // LANES):
        here = pl.ds(tile * LANES, LANES)
        rows_b[here, PAD : PAD + 8] = xyz_ref[:, here].T

    def gather(index, _):
        base = pl.multiple_of(index * 16, 16)
        for i in range(16):
            rows_c[pl.ds(base + i, 1), :] = rows_b[pl.ds(perm_ref[base + i], 1), :]
        return 0

    lax.fori_loop(0, count // 16, gather, 0)
    for tile in range(count // LANES):
        here = rows_c[pl.ds(tile * LANES, LANES), :].T
        cot_out[tile] = here[:width]
        xyz_out[tile] = here[PAD : PAD + 8]


def node_rows(slab, perm, xyz, cotangent):
    count = cotangent.shape[1]
    width = cotangent.shape[0]
    tiles = count // LANES
    return pl.pallas_call(
        node_rows_body,
        out_shape=[
            jax.ShapeDtypeStruct((tiles, 8, LANES), jnp.float32),
            jax.ShapeDtypeStruct((tiles, width, LANES), jnp.float32),
        ],
        in_specs=[pl.BlockSpec(memory_space=pltpu.SMEM)] * 2 + [pl.BlockSpec(memory_space=pltpu.VMEM)] * 2,
        out_specs=[pl.BlockSpec(memory_space=pltpu.VMEM)] * 2,
        scratch_shapes=[pltpu.VMEM((count, LANES), jnp.float32)] * 3,
        compiler_params=pltpu.CompilerParams(vmem_limit_bytes=VMEM),
    )(slab, perm, xyz, cotangent)


def pick_body(slot_ref, table_ref, out_ref, rows_a, rows_b):
    blocks, width, span = table_ref.shape
    count = out_ref.shape[1]
    for block in range(blocks):
        for tile in range(span // LANES):
            rows_a[pl.ds(block * span + tile * LANES, LANES), :width] = table_ref[
                block, :, pl.ds(tile * LANES, LANES)
            ].T

    def gather(index, _):
        base = pl.multiple_of(index * 16, 16)
        for i in range(16):
            rows_b[pl.ds(base + i, 1), :] = rows_a[pl.ds(slot_ref[base + i], 1), :]
        return 0

    lax.fori_loop(0, count // 16, gather, 0)
    for tile in range(count // LANES):
        here = pl.ds(tile * LANES, LANES)
        out_ref[:, here] = rows_b[here, :].T[:width]


def pick(slots, table):
    blocks, width, span = table.shape
    count = slots.shape[0]
    return pl.pallas_call(
        pick_body,
        out_shape=jax.ShapeDtypeStruct((width, count), jnp.float32),
        in_specs=[pl.BlockSpec(memory_space=pltpu.SMEM), pl.BlockSpec(memory_space=pltpu.VMEM)],
        out_specs=pl.BlockSpec(memory_space=pltpu.VMEM),
        scratch_shapes=[
            pltpu.VMEM((blocks * span, LANES), jnp.float32),
            pltpu.VMEM((count, LANES), jnp.float32),
        ],
        compiler_params=pltpu.CompilerParams(vmem_limit_bytes=VMEM),
    )(slots, table)


class Links:
    def __init__(self, nodes, ctrs):
        self.nodes, self.ctrs = nodes, ctrs
        self.node, self.ctr = lax.axis_index("node"), lax.axis_index("ctr")
        self.me = self.node * ctrs + self.ctr

    def on_node(self, hop):
        return (lax.rem(self.node + hop, self.nodes), self.ctr)

    def on_ctr(self, hop):
        return (self.node, lax.rem(self.ctr + hop, self.ctrs))

    def anyone(self, hop):
        other = lax.rem(self.me + hop, self.nodes * self.ctrs)
        return (other // self.ctrs, lax.rem(other, self.ctrs))

    def meet(self, targets):
        barrier = pltpu.get_barrier_semaphore()
        for target in targets:
            pl.semaphore_signal(barrier, inc=1, device_id=target, device_id_type=MESH)
        pl.semaphore_wait(barrier, len(targets))

    def node_hops(self):
        return range(1, self.nodes)

    def ctr_hops(self):
        return range(1, self.ctrs)

    def meet_sides(self):
        self.meet([self.on_node(h) for h in self.node_hops()] + [self.on_ctr(h) for h in self.ctr_hops()])

    def meet_all(self):
        self.meet([self.anyone(h) for h in range(1, self.nodes * self.ctrs)])


def send(source, target, sems, index, device):
    copy = pltpu.make_async_remote_copy(
        src_ref=source,
        dst_ref=target,
        send_sem=sems[0].at[index],
        recv_sem=sems[1].at[index],
        device_id=device,
        device_id_type=MESH,
    )
    copy.start()
    return copy


def finish(copies):
    for copy in copies:
        copy.wait()


def comm_call(body, nodes, ctrs, out_shape, scratch, collective, *args):
    return pl.pallas_call(
        functools.partial(body, nodes, ctrs),
        out_shape=out_shape,
        in_specs=[pl.BlockSpec(memory_space=pltpu.VMEM)] * len(args),
        out_specs=jax.tree.map(lambda _: pl.BlockSpec(memory_space=pltpu.VMEM), out_shape),
        scratch_shapes=scratch,
        compiler_params=pltpu.CompilerParams(
            collective_id=collective, has_side_effects=True, vmem_limit_bytes=VMEM
        ),
    )(*args)


def dma_pair(count):
    return [pltpu.SemaphoreType.DMA((count,))] * 2


def surface_body(nodes, ctrs, own_ref, all_ref, *sems):
    links = Links(nodes, ctrs)
    links.meet_sides()
    mine = all_ref.at[links.ctr, links.node]
    copies = [send(own_ref, mine, sems, h - 1, links.on_node(h)) for h in links.node_hops()]
    all_ref[links.ctr, links.node] = own_ref[...]
    finish(copies)
    whole = all_ref.at[links.ctr]
    finish([send(whole, whole, sems, nodes - 2 + h, links.on_ctr(h)) for h in links.ctr_hops()])


def node_body(nodes, ctrs, own_ref, all_ref, *sems):
    links = Links(nodes, ctrs)
    links.meet([links.on_node(h) for h in links.node_hops()])
    mine = all_ref.at[links.node]
    copies = [send(own_ref, mine, sems, h - 1, links.on_node(h)) for h in links.node_hops()]
    all_ref[links.node] = own_ref[...]
    finish(copies)


def cross_body(nodes, ctrs, own_ref, node_ref, ctr_ref, *sems):
    links = Links(nodes, ctrs)
    links.meet_sides()
    copies = [send(own_ref, node_ref.at[links.node], sems, h - 1, links.on_node(h)) for h in links.node_hops()]
    copies += [
        send(own_ref, ctr_ref.at[links.ctr], sems, nodes - 2 + h, links.on_ctr(h)) for h in links.ctr_hops()
    ]
    node_ref[links.node] = own_ref[...]
    ctr_ref[links.ctr] = own_ref[...]
    finish(copies)


def reduced(links, part_ref, landing, sems):
    copies = []
    for h in links.node_hops():
        device = links.on_node(h)
        copies.append(send(part_ref.at[device[0]], landing.at[h - 1], sems, h - 1, device))
    total = part_ref[links.node]
    for h, copy in zip(links.node_hops(), copies):
        copy.wait()
        total = total + landing[h - 1]
    return total


def shared(links, values, own, everyone, sems):
    own[...] = jnp.concatenate(
        [jnp.broadcast_to(v, (v.shape[0], LANES // len(values))) for v in values], axis=1
    )
    hops = range(1, links.nodes * links.ctrs)
    copies = [send(own, everyone.at[links.me], sems, h - 1, links.anyone(h)) for h in hops]
    everyone[links.me] = own[...]
    finish(copies)
    total = jnp.sum(everyone[...], axis=0)
    step = LANES // len(values)
    return [total[:, i * step : i * step + 1] for i in range(len(values))]


def rowsum(value):
    return jnp.sum(value, axis=1, keepdims=True)


def pulled_body(nodes, ctrs, part_ref, own_ref, cols_ref, landing, s0, s1, t0, t1):
    links = Links(nodes, ctrs)
    links.meet_sides()
    own_ref[...] = reduced(links, part_ref, landing, (s0, s1))
    copies = [
        send(own_ref, cols_ref.at[links.ctr], (t0, t1), h - 1, links.on_ctr(h)) for h in links.ctr_hops()
    ]
    cols_ref[links.ctr] = own_ref[...]
    finish(copies)


def first_body(
    nodes, ctrs, part_ref, pulled_ref, pulled_cols, resid_ref, dir_cols, scal_ref,
    landing, cols, own0, every0, own1, every1, s0, s1, t0, t1, u0, u1, v0, v1,
):
    links = Links(nodes, ctrs)
    links.meet_all()
    image = reduced(links, part_ref, landing, (s0, s1))
    pulled = pulled_ref[...]
    norm, curve = shared(
        links, [rowsum(pulled * pulled), rowsum(pulled * image)], own0, every0, (t0, t1)
    )
    alpha = norm / curve
    resid = pulled - alpha * image
    resid_ref[...] = resid
    copies = [
        send(resid_ref, cols.at[links.ctr], (u0, u1), h - 1, links.on_ctr(h)) for h in links.ctr_hops()
    ]
    cols[links.ctr] = resid
    (after,) = shared(links, [rowsum(resid * resid)], own1, every1, (v0, v1))
    ratio = after / norm
    finish(copies)
    dir_cols[...] = cols[...] + ratio[None] * pulled_cols[...]
    step = LANES // 4
    wide = (alpha.shape[0], step)
    scal_ref[...] = jnp.concatenate(
        [jnp.broadcast_to(v, wide) for v in (alpha, ratio, after, norm)], axis=1
    )


def second_body(
    nodes, ctrs, part_ref, pulled_ref, resid_ref, scal_ref, out_ref,
    landing, final, own0, every0, s0, s1, t0, t1, u0, u1,
):
    links = Links(nodes, ctrs)
    links.meet_all()
    image = reduced(links, part_ref, landing, (s0, s1))
    pulled, resid, scal = pulled_ref[...], resid_ref[...], scal_ref[...]
    step = LANES // 4
    alpha, ratio, after = (scal[:, i * step : i * step + 1] for i in range(3))
    direction = resid + ratio * pulled
    (curve,) = shared(links, [rowsum(direction * image)], own0, every0, (t0, t1))
    second = after / curve
    final[...] = jnp.concatenate(
        [alpha * pulled + second * direction, resid - second * image], axis=0
    )
    copies = [
        send(final, out_ref.at[links.node], (u0, u1), h - 1, links.on_node(h)) for h in links.node_hops()
    ]
    out_ref[links.node] = final[...]
    finish(copies)


def local(nodes, ctrs, surface_xyz, centre_idx, volume_xyz, slab_ids, cotangent):
    width = cotangent.shape[0]
    owned = centre_idx.shape[0]
    total = owned * nodes
    here = lax.axis_index("node")
    f32 = jnp.float32
    vmem = lambda *shape: pltpu.VMEM(shape, f32)
    out = lambda *shape: jax.ShapeDtypeStruct(shape, f32)
    devices = nodes * ctrs

    slab = slab_ids % volume_xyz.shape[1]
    node_perm = lax.sort(sort_key(volume_xyz)) % volume_xyz.shape[1]
    volume_points = jnp.concatenate(
        [scaled(volume_xyz), jnp.zeros((4, volume_xyz.shape[1]), f32)], axis=0
    )
    volume_points = jnp.concatenate([volume_points[4:], volume_points[:4]], axis=0)
    node_points, node_vec = node_rows(slab, node_perm, volume_points, cotangent)

    rows = surface_xyz.shape[1] // LANES
    surface = comm_call(
        surface_body, nodes, ctrs, out(ctrs, nodes, 3, rows, LANES), dma_pair(nodes + ctrs - 2), 0,
        surface_xyz.reshape(3, rows, LANES),
    )
    surface = surface.transpose(2, 1, 0, 3, 4).reshape(3, -1)
    mine = lookup(surface, centre_idx)

    plane = comm_call(
        node_body, nodes, ctrs, out(nodes, 8, owned), dma_pair(nodes - 1), 1,
        jnp.pad(mine, ((0, 5), (0, 0))),
    )[:, :3]
    plane = plane.transpose(1, 0, 2).reshape(3, total)
    perm = lax.sort(sort_key(plane)) % total
    by_owner = perm.reshape(owned // LANES, nodes, LANES)
    own_perm = lax.dynamic_index_in_dim(by_owner, here, 1, False).reshape(owned)
    sorted_mine = scaled(lookup(plane, own_perm))
    sorted_mine = jnp.concatenate([jnp.zeros_like(sorted_mine), sorted_mine], axis=0)
    row_points, col_points = comm_call(
        cross_body, nodes, ctrs, (out(nodes, 8, owned), out(ctrs, 8, owned)), dma_pair(nodes + ctrs - 2), 2,
        sorted_mine,
    )
    row_points = row_points.transpose(1, 0, 2).reshape(8, total)[4:]
    left = row_features(row_points)
    tiles = owned // LANES

    def tiled(value):
        shape = (value.shape[0], value.shape[1], tiles, LANES)
        return value.reshape(shape).transpose(0, 2, 1, 3).reshape(-1, shape[1], LANES)

    col_tiles = tiled(col_points)
    groups = boxes(row_points, GROUP)
    flat = lambda value: value.transpose(1, 0, 2).reshape(8, -1)[4:]
    node_lists = near_lists(boxes(flat(node_points), LANES), groups)
    col_lists = near_lists(boxes(flat(col_tiles), LANES), groups)

    places = jnp.arange(total, dtype=jnp.int32)
    hit = (by_owner.transpose(1, 0, 2).reshape(total) // LANES)[None, :] == (
        here * tiles + jnp.arange(tiles, dtype=jnp.int32)
    )[:, None]
    spots = jnp.concatenate(
        [jnp.where(hit, (places // LANES)[None, :], 0), jnp.where(hit, (places % LANES)[None, :], 0)], axis=0
    ).astype(jnp.bfloat16)
    lane = (
        by_owner.transpose(1, 0, 2).reshape(total)[:, None] % LANES == jnp.arange(LANES, dtype=jnp.int32)[None, :]
    ).astype(jnp.bfloat16)
    spots = jnp.dot(spots, lane, preferred_element_type=f32).astype(jnp.int32)
    slots = (spots[:tiles] * LANES + spots[tiles:]).reshape(owned)

    part = apply_kernel(node_lists, left, node_points, node_vec, nodes)
    own_shape, small = out(width, owned), vmem(width, LANES)
    landing = vmem(nodes - 1, width, owned)
    every = vmem(devices, width, LANES)
    pulled, pulled_cols = comm_call(
        pulled_body, nodes, ctrs, (own_shape, out(ctrs, width, owned)),
        [landing] + dma_pair(nodes - 1) + dma_pair(ctrs - 1), 3, part,
    )
    part = apply_kernel(col_lists, left, col_tiles, tiled(pulled_cols), nodes)
    resid, dir_cols, scal = comm_call(
        first_body, nodes, ctrs, (own_shape, out(ctrs, width, owned), out(width, LANES)),
        [landing, vmem(ctrs, width, owned), small, every, small, every]
        + dma_pair(nodes - 1) + dma_pair(devices - 1) + dma_pair(ctrs - 1) + dma_pair(devices - 1),
        4, part, pulled, pulled_cols,
    )
    part = apply_kernel(col_lists, left, col_tiles, tiled(dir_cols), nodes)
    final = comm_call(
        second_body, nodes, ctrs, out(nodes, 2 * width, owned),
        [landing, vmem(2 * width, owned), small, every]
        + dma_pair(nodes - 1) + dma_pair(devices - 1) + dma_pair(nodes - 1),
        5, part, pulled, resid, scal,
    )
    final = pick(slots, final)
    return final[:width], final[width:]


def solution(mesh):
    return jax.shard_map(
        functools.partial(local, mesh.shape["node"], mesh.shape["ctr"]),
        mesh=mesh,
        in_specs=(
            P(None, ("node", "ctr")),
            P(("node", "ctr")),
            P(None, "node"),
            P("node"),
            P(None, "node"),
        ),
        out_specs=(P(None, ("node", "ctr")), P(None, ("node", "ctr"))),
        check_vma=False,
    )
```

time: 446 us -> 283 us (0.63)
  blocking collectives: 86.5 us -> 0 us
  waiting for transfers between devices: 70.1 us -> 0 us
  between operations: 14.1 us -> 1.11 us
  other arithmetic: 12.9 us -> 23 us
    all_gather x5 -> x0, waiting for transfers between devices: 70 us -> none  [the longest x1 55.6 us: local(): image_all = lax.all_gather(image, everyone, axis=0)]
    all_gather x1 -> x0, blocking collectives: 47.9 us -> none  [local(): surface = lax.all_gather(surface_xyz.reshape(-1), everyone, axis=0)]
    psum x1 -> x0, blocking collectives: 38.5 us -> none  [local(): curve = lax.psum(jnp.sum(direction * image, axis=1), everyone)]
    sort x0 -> x2, other arithmetic: none -> 12.5 us  [the longest x1 6.77 us: local(): perm = lax.sort(sort_key(plane)) % total]
    unnamed x27 -> x8, local copies, waits for them, and re-layouts: 7 us -> 0.82 us
    pallas_call x6 -> x11, Pallas kernels: 248 us -> 247 us  [the longest x6 133 us: comm_call(): pl.pallas_call(functools.partial(body, nodes, ctrs), out_shape=out_shape,...]
  transfers between devices with their start and end apart: 5 -> 0, of which waited for: 3 -> 0; matrix products, arithmetic and copies ran while one was open for 2% -> 0% of each run, Pallas kernels for 32% -> 0%
where the time goes in v1:
time: 283 us; the launch traced here: 280 us
  Pallas kernels  247 us (87%)
  other arithmetic  23 us (8%)
  local copies, waits for them, and re-layouts  5.17 us (2%)
  matrix products  4.1 us (1%)
    pallas_call x6, Pallas kernels, comm_call(): pl.pallas_call(functools.partial(body, nodes, ctrs), out_shape=out_shape,...  133 us
    pallas_call x3, Pallas kernels, apply_kernel(): pl.pallas_call(apply_body, out_shape=jax.ShapeDtypeStruct((owners, width,...  98.2 us
    pallas_call x1, Pallas kernels, node_rows(): pl.pallas_call(node_rows_body, out_shape=[jax.ShapeDtypeStruct((tiles, 8,...  12.3 us
    sort x1, other arithmetic, local(): perm = lax.sort(sort_key(plane)) % total  6.77 us
    sort x1, other arithmetic, local(): node_perm = lax.sort(sort_key(volume_xyz)) % volume_xyz.shape[1]  5.78 us

profile of v1, /device:TPU:0, one launch (start us, length us, event | category | flops | bytes accessed | tf_op | source)
XLA Modules:
  0.0 280.0 jit_solution(3724678748110909486)
XLA Ops:
  1.4 0.8 copy.101
  2.2 17.8 %shard_map.68 = f32[4,8,3,16,128]{4,3,2,1,0:T(8,128)S(1)} custom-call(f32[3,16,128]{2,1,0:T(8,128)S(1)} %bitcast.124), custom_call_target="tpu_custom_call" | custom-call | tf_op jit(solution)/shard_map/pallas_call | solution.py:353
  21.0 1.7 select_reduce_fusion.3
  22.7 8.9 %shard_map.69 = f32[8,8,1024]{2,1,0:T(8,128)S(1)} custom-call(f32[8,1024]{1,0:T(8,128)S(1)} %pad.14.own_ref), custom_call_target="tpu_custom_call" | custom-call | tf_op jit(solution)/shard_map/pallas_call | solution.py:353
  31.9 6.8 %sort.28 = (s32[8192]{0:T(1024)S(1)}, s32[8192]{0:T(1024)}) sort(s32[8192]{0:T(1024)S(1)} %fusion.39, s32[8192]{0:T(1024)S(1)} %iota.68), dimensions={0}, to_apply=%region_1.2 | sort | flops 106496 | bytes 131072 | tf_op jit(solution)/shard_map/sort | solution.py:524
  38.9 1.3 fusion.5
  40.3 5.8 %sort.29 = (s32[4096]{0:T(1024)S(1)}, s32[4096]{0:T(1024)}) sort(s32[4096]{0:T(1024)S(1)} %fusion.57, s32[4096]{0:T(1024)S(1)} %iota.72), dimensions={0}, to_apply=%region_11.12 | sort | flops 49152 | bytes 65536 | tf_op jit(solution)/shard_map/sort | solution.py:504
  46.3 12.3 %shard_map.71 = (f32[32,8,128]{2,1,0:T(8,128)S(1)}, f32[32,12,128]{2,1,0:T(8,128)S(1)}) custom-call(s32[4096]{0:T(1024)S(1)} %get-tuple-element.66.slab_ref, s32[4096]{0:T(1024)S(1)} %get-tuple-element.65.perm_ref, f32[8,4096]{1,0:T(8,128)S(1)} %maximum_maximum_fusion.xyz_ref, f32[12,4096]{1,0:T(8,128)S(1)} %copy-done), custom_call_target="tpu_custom_call" | custom-call | tf_op jit(solution)/shard_map/pallas_call | solution.py:249
  59.2 0.9 select_reduce_fusion.2
  60.2 11.0 %shard_map.70 = (f32[8,8,1024]{2,1,0:T(8,128)S(1)}, f32[4,8,1024]{2,1,0:T(8,128)S(1)}) custom-call(f32[8,1024]{1,0:T(8,128)S(1)} %maximum_maximum_fusion.1.own_ref), custom_call_target="tpu_custom_call" | custom-call | tf_op jit(solution)/shard_map/pallas_call | solution.py:353
  72.6 1.4 select_reduce_fusion.1.order
  74.9 0.8 constant_dynamic-update-slice_fusion.3
  75.6 0.8 constant_dynamic-update-slice_fusion.2
  76.4 0.8 constant_dynamic-update-slice_fusion.1
  77.9 0.8 fusion.20
  78.7 2.0 copy.59
  80.9 1.4 select_reduce_fusion.order
  82.4 37.2 %shard_map.72.part_ref = f32[8,12,1024]{2,1,0:T(8,128)S(1)} custom-call(s32[32]{0:T(128)S(1)} %get-tuple-element.34.count, s32[32,256]{1,0:T(8,128)S(1)} %select_reduce_fusion.order, bf16[8192,48]{1,0:T(8,128)(2,1)S(1)} %bitcast.116, f32[32,8,128]{2,1,0:T(8,128)S(1)} %get-tuple-element.19.beta_ref, f32[32,16,128]{2,1,0:T(8,128)S(1)} %pad.15.vec_ref), custom_call_target="tpu_custom_call" | custom-call | tf_op jit(solution)/shard_map/pallas_call | solution.py:194
  119.5 20.3 %shard_map.73 = (f32[12,1024]{1,0:T(8,128)S(1)}, f32[4,12,1024]{2,1,0:T(8,128)S(1)}) custom-call(f32[8,12,1024]{2,1,0:T(8,128)S(1)} %shard_map.72.part_ref), custom_call_target="tpu_custom_call" | custom-call | tf_op jit(solution)/shard_map/pallas_call | solution.py:353
  140.0 30.5 %shard_map.74.part_ref = f32[8,12,1024]{2,1,0:T(8,128)S(1)} custom-call(s32[32]{0:T(128)S(1)} %get-tuple-element.36.count, s32[32,256]{1,0:T(8,128)S(1)} %select_reduce_fusion.1.order, bf16[8192,48]{1,0:T(8,128)(2,1)S(1)} %bitcast.117, f32[32,8,128]{2,1,0:T(8,128)S(1)} %bitcast.121, f32[32,16,128]{2,1,0:T(8,128)S(1)} %pad.16.vec_ref), custom_call_target="tpu_custom_call" | custom-call | tf_op jit(solution)/shard_map/pallas_call | solution.py:194
  170.5 37.3 %shard_map.75 = (f32[12,1024]{1,0:T(8,128)S(1)}, f32[4,12,1024]{2,1,0:T(8,128)S(1)}, f32[12,128]{1,0:T(8,128)S(1)}) custom-call(f32[8,12,1024]{2,1,0:T(8,128)S(1)} %shard_map.74.part_ref, f32[12,1024]{1,0:T(8,128)S(1)} %get-tuple-element.22.pulled_ref, f32[4,12,1024]{2,1,0:T(8,128)S(1)} %get-tuple-element.21.pulled_cols), custom_call_target="tpu_custom_call" | custom-call | tf_op jit(solution)/shard_map/pallas_call | solution.py:353
  207.9 30.5 %shard_map.76.part_ref = f32[8,12,1024]{2,1,0:T(8,128)S(1)} custom-call(s32[32]{0:T(128)S(1)} %get-tuple-element.36.count, s32[32,256]{1,0:T(8,128)S(1)} %select_reduce_fusion.1.order, bf16[8192,48]{1,0:T(8,128)(2,1)S(1)} %bitcast.118, f32[32,8,128]{2,1,0:T(8,128)S(1)} %bitcast.122, f32[32,16,128]{2,1,0:T(8,128)S(1)} %pad.17.vec_ref), custom_call_target="tpu_custom_call" | custom-call | tf_op jit(solution)/shard_map/pallas_call | solution.py:194
  238.4 37.9 %shard_map.77.table_ref = f32[8,24,1024]{2,1,0:T(8,128)S(1)} custom-call(f32[8,12,1024]{2,1,0:T(8,128)S(1)} %shard_map.76.part_ref, f32[12,1024]{1,0:T(8,128)S(1)} %get-tuple-element.22.pulled_ref, f32[12,1024]{1,0:T(8,128)S(1)} %get-tuple-element.24.resid_ref, f32[12,128]{1,0:T(8,128)S(1)} %get-tuple-element.25.scal_ref), custom_call_target="tpu_custom_call" | custom-call | tf_op jit(solution)/shard_map/pallas_call | solution.py:353
  276.3 3.0 %shard_map.78 = f32[24,1024]{1,0:T(8,128)S(1)} custom-call(s32[1024]{0:T(1024)S(1)} %fusion.67.slot_ref, f32[8,24,1024]{2,1,0:T(8,128)S(1)} %shard_map.77.table_ref), custom_call_target="tpu_custom_call" | custom-call | tf_op jit(solution)/shard_map/pallas_call | solution.py:286
  (73 shorter events, 7.3 us)
Async XLA Ops:
  22.7 17.5 %copy-start.1 = (f32[3,4096]{1,0:T(4,128)S(1)}, f32[3,4096]{1,0:T(4,128)}, u32[]{:S(2)}) copy-start(f32[3,4096]{1,0:T(4,128)} %param.7) | copy-start | bytes 147460
  22.7 23.4 %copy-start.2 = (s32[4096]{0:T(1024)S(1)}, s32[4096]{0:T(1024)}, u32[]{:S(2)}) copy-start(s32[4096]{0:T(1024)} %param.8) | copy-start | bytes 49156
  22.7 23.6 %copy-start = (f32[12,4096]{1,0:T(8,128)S(1)}, f32[12,4096]{1,0:T(8,128)}, u32[]{:S(2)}) copy-start(f32[12,4096]{1,0:T(8,128)} %cot_ref.1) | copy-start | bytes 589828

commit v2 on v1

--- a/solution.py
+++ b/solution.py
@@ -104,34 +104,34 @@
     order = jnp.sum(
         jnp.where(place[:, :, None] == every[None, None, :], every[None, :, None], 0), axis=1
     )
-    return count, order
-
-
-def apply_body(count, order, left_ref, beta_ref, vec_ref, out_ref, acc, right, vec, items, q0, q1, k0, k1):
+    return count, jnp.pad((order * GROUP).reshape(-1), (0, size))
+
+
+def apply_body(count, order, left_ref, right_ref, vec_ref, out_ref, acc, vec, items, q0, q1, k0, k1):
     rows = left_ref.shape[0]
-    tiles = beta_ref.shape[0]
+    tiles = right_ref.shape[0]
     span = GROUP * BATCH
+    half = span // 2
+    banks, width, deep = vec_ref.shape[:3]
     acc[...] = jnp.zeros_like(acc)
     for ref in (q0, q1, k0, k1):
         ref[...] = jnp.zeros_like(ref)
 
-    def prepare(tile, _):
-        right[tile] = right_factor(beta_ref[tile])
-        parts = two_parts(vec_ref[tile])
-        vec[tile] = jnp.concatenate([parts, parts], axis=1)
-        return 0
-
-    lax.fori_loop(0, tiles, prepare, 0)
-    right[tiles] = jnp.zeros_like(right[tiles])
+    blank = jnp.zeros((PAD - width, LANES), jnp.float32)
+    for bank in range(banks):
+        for at in range(deep):
+            parts = two_parts(jnp.concatenate([vec_ref[bank, :, at, :], blank], axis=0))
+            vec[bank * deep + at] = jnp.concatenate([parts, parts], axis=1)
     vec[tiles] = jnp.zeros_like(vec[tiles])
 
-    nothing = tiles * rows
+    groups = rows // GROUP
+    nothing = tiles * groups
     for index in range(2 * PAIR):
         items[index] = nothing
 
     def fill(tile, at):
         def one(batch, at):
-            items[at] = tile * rows + batch * BATCH
+            items[at] = tile * groups + batch * BATCH
             return at + 1
 
         return lax.fori_loop(0, (count[tile] + BATCH - 1) // BATCH, one, at)
@@ -140,34 +140,44 @@
     for index in range(4 * PAIR):
         items[end + index] = nothing
 
+    first_half = lax.broadcasted_iota(jnp.int32, (half, LANES), 1) < LANES // 2
+
     def item(index):
         code = items[index]
-        tile = code // rows
-        first = code - tile * rows
-        listed = jnp.minimum(tile, tiles - 1)
-        return tile, [pl.multiple_of(order[listed, first + i] * GROUP, GROUP) for i in range(BATCH)]
+        tile = lax.div(code, groups)
+        return tile, jnp.minimum(tile, tiles - 1), [
+            pl.multiple_of(order[code + i], GROUP) for i in range(BATCH)
+        ]
+
+    def rows_at(places):
+        return jnp.concatenate([left_ref[pl.ds(place, GROUP), :] for place in places], axis=0)
 
     def step(index, q_in, q_out, k_in, k_out):
         for unit in range(PAIR):
-            tile, places = item(index * PAIR + unit)
+            tile, _, places = item(index * PAIR + unit)
             part = lax.dot_general(
                 k_in[pl.ds(unit * span, span), :], vec[tile], NT, preferred_element_type=jnp.float32
             )
             for j, place in enumerate(places):
                 acc[pl.ds(place, GROUP), :] += part[j * GROUP : (j + 1) * GROUP]
-        q = jnp.minimum(jnp.maximum(q_in[...], 1e-30), 1.0)
-        s = q * lax.rsqrt(q)
-        w = 1.0 - s
-        w2 = w * w
-        k = (w2 * w2) * (0.25 + s)
-        hi = k.astype(jnp.bfloat16)
-        k_out[:, :LANES] = hi
-        k_out[:, LANES:] = (k - hi.astype(jnp.float32)).astype(jnp.bfloat16)
         for unit in range(PAIR):
-            tile, places = item((index + 2) * PAIR + unit)
-            left = jnp.concatenate([left_ref[pl.ds(place, GROUP), :] for place in places], axis=0)
-            q_out[pl.ds(unit * span, span), :] = jnp.dot(
-                left, right[tile], preferred_element_type=jnp.float32
+            q = jnp.minimum(jnp.maximum(q_in[pl.ds(unit * half, half), :], 1e-30), 1.0)
+            s = q * lax.rsqrt(q)
+            w = 1.0 - s
+            w2 = w * w
+            k = (w2 * w2) * (0.25 + s)
+            hi = k.astype(jnp.bfloat16)
+            lo = (k - hi.astype(jnp.float32)).astype(jnp.bfloat16)
+            for side in range(2):
+                here = pl.ds(unit * span + side * half, half)
+                lanes = slice(side * LANES, (side + 1) * LANES)
+                k_out[here, :LANES] = hi[:, lanes]
+                k_out[here, LANES:] = lo[:, lanes]
+        for unit in range(PAIR):
+            _, listed, places = item((index + 2) * PAIR + unit)
+            left = jnp.where(first_half, rows_at(places[: BATCH // 2]), rows_at(places[BATCH // 2 :]))
+            q_out[pl.ds(unit * half, half), :] = jnp.dot(
+                left, right_ref[listed], preferred_element_type=jnp.float32
             )
 
     def two_steps(index, _):
@@ -178,36 +188,89 @@
     steps = (end - 2 * PAIR + PAIR - 1) // PAIR + 2
     lax.fori_loop(0, (steps + 1) // 2, two_steps, 0)
 
-    owners, width, owned = out_ref.shape
+    owners, _, high, _ = out_ref.shape
     for owner in range(owners):
-        total = acc[pl.ds(owner * owned, owned), :].T
-        out_ref[owner] = 4.0 * (total[:width] + total[PAD : PAD + width])
-
-
-def apply_kernel(lists, left, beta, vec, owners):
+        for at in range(high):
+            total = acc[pl.ds((owner * high + at) * LANES, LANES), :].T
+            out_ref[owner, :, at, :] = 4.0 * (total[:width] + total[PAD : PAD + width])
+
+
+def apply_kernel(lists, left, right, vec, owners):
     count, order = lists
     rows = left.shape[0]
-    tiles = beta.shape[0]
+    tiles = right.shape[0]
     width = vec.shape[1]
-    vec = jnp.pad(vec, ((0, 0), (0, PAD - width), (0, 0)))
     wide = PAIR * GROUP * BATCH
     return pl.pallas_call(
         apply_body,
-        out_shape=jax.ShapeDtypeStruct((owners, width, rows // owners), jnp.float32),
+        out_shape=jax.ShapeDtypeStruct((owners, width, rows // owners // LANES, LANES), jnp.float32),
         in_specs=[pl.BlockSpec(memory_space=pltpu.SMEM)] * 2 + [pl.BlockSpec(memory_space=pltpu.VMEM)] * 3,
         out_specs=pl.BlockSpec(memory_space=pltpu.VMEM),
         scratch_shapes=[
             pltpu.VMEM((rows, 2 * PAD), jnp.float32),
-            pltpu.VMEM((tiles + 1, 48, LANES), jnp.bfloat16),
             pltpu.VMEM((tiles + 1, 2 * PAD, 2 * LANES), jnp.bfloat16),
             pltpu.SMEM((tiles * (rows // (GROUP * BATCH)) + 8 * PAIR,), jnp.int32),
-            pltpu.VMEM((wide, LANES), jnp.float32),
-            pltpu.VMEM((wide, LANES), jnp.float32),
+            pltpu.VMEM((wide // 2, 2 * LANES), jnp.float32),
+            pltpu.VMEM((wide // 2, 2 * LANES), jnp.float32),
             pltpu.VMEM((wide, 2 * LANES), jnp.bfloat16),
             pltpu.VMEM((wide, 2 * LANES), jnp.bfloat16),
         ],
         compiler_params=pltpu.CompilerParams(vmem_limit_bytes=VMEM),
-    )(count, order, left, beta, vec)
+    )(count, order, left, right, vec)
+
+
+def factor_body(row_ref, col_ref, node_ref, left_ref, col_out, node_out):
+    blocks, _, span = row_ref.shape
+    blank = jnp.zeros((16, LANES), jnp.float32)
+    for block in range(blocks):
+        for at in range(span // LANES):
+            group = row_ref[block, :, pl.ds(at * LANES, LANES)]
+            row = lax.broadcasted_iota(jnp.int32, group.shape, 0)
+            place = jnp.where((row >= 4) & (row < 7), group, 0.0)
+            square = jnp.sum(place * place, axis=0, keepdims=True)
+            alpha = jnp.where(row == 0, 1.0, jnp.where(row == 7, square, -2.0 * place))
+            a1 = rounded(alpha)
+            a2 = rounded(alpha - a1)
+            a3 = alpha - a1 - a2
+            parts = [a1, a1, a2, a2, a1, a3, blank]
+            left_ref[pl.ds((block * (span // LANES) + at) * LANES, LANES), :] = (
+                jnp.concatenate(parts + parts, axis=0).T.astype(jnp.bfloat16)
+            )
+
+    def fill(source, target):
+        blocks, _, span = source.shape
+        per = span // LANES
+        zero = jnp.zeros((64, LANES), jnp.bfloat16)
+        pad = jnp.zeros((16, LANES), jnp.bfloat16)
+        for block in range(blocks):
+            for at in range(per):
+                right = jnp.concatenate([right_factor(source[block, :, pl.ds(at * LANES, LANES)]), pad], axis=0)
+                target[block * per + at] = jnp.concatenate(
+                    [jnp.concatenate([right, zero], axis=0), jnp.concatenate([zero, right], axis=0)], axis=1
+                )
+
+    fill(col_ref, col_out)
+    fill(node_ref, node_out)
+
+
+def factors(row_points, col_points, node_points):
+    def tiles(points):
+        return points.shape[0] * points.shape[2] // LANES
+
+    def shape(points):
+        return jax.ShapeDtypeStruct((tiles(points), LANES, 2 * LANES), jnp.bfloat16)
+
+    return pl.pallas_call(
+        factor_body,
+        out_shape=[
+            jax.ShapeDtypeStruct((tiles(row_points) * LANES, LANES), jnp.bfloat16),
+            shape(col_points),
+            shape(node_points),
+        ],
+        in_specs=[pl.BlockSpec(memory_space=pltpu.VMEM)] * 3,
+        out_specs=[pl.BlockSpec(memory_space=pltpu.VMEM)] * 3,
+        compiler_params=pltpu.CompilerParams(vmem_limit_bytes=VMEM),
+    )(row_points, col_points, node_points)
 
 
 def node_rows_body(slab_ref, perm_ref, xyz_ref, cot_ref, xyz_out, cot_out, rows_a, rows_b, rows_c):
@@ -238,8 +301,8 @@
     lax.fori_loop(0, count // 16, gather, 0)
     for tile in range(count // LANES):
         here = rows_c[pl.ds(tile * LANES, LANES), :].T
-        cot_out[tile] = here[:width]
-        xyz_out[tile] = here[PAD : PAD + 8]
+        cot_out[0, :, tile, :] = here[:width]
+        xyz_out[0, :, pl.ds(tile * LANES, LANES)] = here[PAD : PAD + 8]
 
 
 def node_rows(slab, perm, xyz, cotangent):
@@ -249,8 +312,8 @@
     return pl.pallas_call(
         node_rows_body,
         out_shape=[
-            jax.ShapeDtypeStruct((tiles, 8, LANES), jnp.float32),
-            jax.ShapeDtypeStruct((tiles, width, LANES), jnp.float32),
+            jax.ShapeDtypeStruct((1, 8, count), jnp.float32),
+            jax.ShapeDtypeStruct((1, width, tiles, LANES), jnp.float32),
         ],
         in_specs=[pl.BlockSpec(memory_space=pltpu.SMEM)] * 2 + [pl.BlockSpec(memory_space=pltpu.VMEM)] * 2,
         out_specs=[pl.BlockSpec(memory_space=pltpu.VMEM)] * 2,
@@ -260,13 +323,11 @@
 
 
 def pick_body(slot_ref, table_ref, out_ref, rows_a, rows_b):
-    blocks, width, span = table_ref.shape
+    blocks, width, deep, _ = table_ref.shape
     count = out_ref.shape[1]
     for block in range(blocks):
-        for tile in range(span // LANES):
-            rows_a[pl.ds(block * span + tile * LANES, LANES), :width] = table_ref[
-                block, :, pl.ds(tile * LANES, LANES)
-            ].T
+        for tile in range(deep):
+            rows_a[pl.ds((block * deep + tile) * LANES, LANES), :width] = table_ref[block, :, tile, :].T
 
     def gather(index, _):
         base = pl.multiple_of(index * 16, 16)
@@ -281,7 +342,7 @@
 
 
 def pick(slots, table):
-    blocks, width, span = table.shape
+    blocks, width, deep, _ = table.shape
     count = slots.shape[0]
     return pl.pallas_call(
         pick_body,
@@ -289,7 +350,7 @@
         in_specs=[pl.BlockSpec(memory_space=pltpu.SMEM), pl.BlockSpec(memory_space=pltpu.VMEM)],
         out_specs=pl.BlockSpec(memory_space=pltpu.VMEM),
         scratch_shapes=[
-            pltpu.VMEM((blocks * span, LANES), jnp.float32),
+            pltpu.VMEM((blocks * deep * LANES, LANES), jnp.float32),
             pltpu.VMEM((count, LANES), jnp.float32),
         ],
         compiler_params=pltpu.CompilerParams(vmem_limit_bytes=VMEM),
@@ -374,7 +435,17 @@
     all_ref[links.ctr, links.node] = own_ref[...]
     finish(copies)
     whole = all_ref.at[links.ctr]
-    finish([send(whole, whole, sems, nodes - 2 + h, links.on_ctr(h)) for h in links.ctr_hops()])
+    last = nodes - 1
+    if ctrs != 4:
+        finish([send(whole, whole, sems, last - 1 + h, links.on_ctr(h)) for h in links.ctr_hops()])
+        return
+    far = lax.rem(links.ctr + 2, 4)
+    near = (links.node, links.ctr + 1 - 2 * lax.rem(links.ctr, 2))
+    across = send(whole, whole, sems, last, (links.node, far))
+    beside = send(whole, whole, sems, last + 1, near)
+    across.wait()
+    other = all_ref.at[far]
+    finish([send(other, other, sems, last + 2, near), beside])
 
 
 def node_body(nodes, ctrs, own_ref, all_ref, *sems):
@@ -410,21 +481,37 @@
     return total
 
 
-def shared(links, values, own, everyone, sems):
-    own[...] = jnp.concatenate(
-        [jnp.broadcast_to(v, (v.shape[0], LANES // len(values))) for v in values], axis=1
-    )
+def wanted(rows, index):
+    row = lax.broadcasted_iota(jnp.int32, (rows, LANES), 0)
+    lane = lax.broadcasted_iota(jnp.int32, (rows, LANES), 1)
+    return lane == row + 32 * index
+
+
+def share_start(links, values, own, everyone, sems):
+    line = 0.0
+    for index, value in enumerate(values):
+        column = jnp.sum(jnp.sum(value, axis=1), axis=1, keepdims=True)
+        line += jnp.sum(
+            jnp.where(wanted(column.shape[0], index), column, 0.0), axis=0, keepdims=True
+        )
+    own[...] = line
     hops = range(1, links.nodes * links.ctrs)
     copies = [send(own, everyone.at[links.me], sems, h - 1, links.anyone(h)) for h in hops]
     everyone[links.me] = own[...]
+    return copies
+
+
+def share_end(copies, count, rows, everyone):
     finish(copies)
-    total = jnp.sum(everyone[...], axis=0)
-    step = LANES // len(values)
-    return [total[:, i * step : i * step + 1] for i in range(len(values))]
-
-
-def rowsum(value):
-    return jnp.sum(value, axis=1, keepdims=True)
+    line = jnp.sum(everyone[...], axis=0)
+    return [
+        jnp.sum(jnp.where(wanted(rows, index), line, 0.0), axis=1, keepdims=True) for index in range(count)
+    ]
+
+
+def spread(column, ref):
+    ref[...] = jnp.broadcast_to(column, ref.shape)
+    return [ref[v : v + 1, :] for v in range(ref.shape[0])]
 
 
 def pulled_body(nodes, ctrs, part_ref, own_ref, cols_ref, landing, s0, s1, t0, t1):
@@ -440,49 +527,55 @@
 
 def first_body(
     nodes, ctrs, part_ref, pulled_ref, pulled_cols, resid_ref, dir_cols, scal_ref,
-    landing, cols, own0, every0, own1, every1, s0, s1, t0, t1, u0, u1, v0, v1,
+    landing, image_ref, cols, line, every, scr0, scr1, s0, s1, t0, t1, u0, u1,
 ):
     links = Links(nodes, ctrs)
     links.meet_all()
     image = reduced(links, part_ref, landing, (s0, s1))
+    image_ref[...] = image
     pulled = pulled_ref[...]
-    norm, curve = shared(
-        links, [rowsum(pulled * pulled), rowsum(pulled * image)], own0, every0, (t0, t1)
-    )
+    told = share_start(
+        links, [pulled * pulled, pulled * image, image * image], line, every, (t0, t1)
+    )
+    copies = [
+        send(image_ref, cols.at[links.ctr], (u0, u1), h - 1, links.on_ctr(h)) for h in links.ctr_hops()
+    ]
+    cols[links.ctr] = image
+    width = pulled_ref.shape[0]
+    norm, curve, square = share_end(told, 3, width, every)
     alpha = norm / curve
-    resid = pulled - alpha * image
-    resid_ref[...] = resid
-    copies = [
-        send(resid_ref, cols.at[links.ctr], (u0, u1), h - 1, links.on_ctr(h)) for h in links.ctr_hops()
-    ]
-    cols[links.ctr] = resid
-    (after,) = shared(links, [rowsum(resid * resid)], own1, every1, (v0, v1))
-    ratio = after / norm
+    ratio = alpha * square / curve - 1.0
+    alphas, ratios = spread(alpha, scr0), spread(ratio, scr1)
+    scal_ref[0] = scr0[...]
+    scal_ref[1] = scr1[...]
+    for v in range(width):
+        resid_ref[v] = pulled_ref[v] - alphas[v] * image_ref[v]
     finish(copies)
-    dir_cols[...] = cols[...] + ratio[None] * pulled_cols[...]
-    step = LANES // 4
-    wide = (alpha.shape[0], step)
-    scal_ref[...] = jnp.concatenate(
-        [jnp.broadcast_to(v, wide) for v in (alpha, ratio, after, norm)], axis=1
-    )
+    for c in range(ctrs):
+        for v in range(width):
+            dir_cols[c, v] = (pulled_cols[c, v] - alphas[v] * cols[c, v]) + ratios[v] * pulled_cols[c, v]
 
 
 def second_body(
     nodes, ctrs, part_ref, pulled_ref, resid_ref, scal_ref, out_ref,
-    landing, final, own0, every0, s0, s1, t0, t1, u0, u1,
+    landing, final, line, every, scr0, s0, s1, t0, t1, u0, u1,
 ):
     links = Links(nodes, ctrs)
     links.meet_all()
     image = reduced(links, part_ref, landing, (s0, s1))
-    pulled, resid, scal = pulled_ref[...], resid_ref[...], scal_ref[...]
-    step = LANES // 4
-    alpha, ratio, after = (scal[:, i * step : i * step + 1] for i in range(3))
-    direction = resid + ratio * pulled
-    (curve,) = shared(links, [rowsum(direction * image)], own0, every0, (t0, t1))
-    second = after / curve
-    final[...] = jnp.concatenate(
-        [alpha * pulled + second * direction, resid - second * image], axis=0
-    )
+    width = pulled_ref.shape[0]
+    alphas = [scal_ref[0, v : v + 1, :] for v in range(width)]
+    ratios = [scal_ref[1, v : v + 1, :] for v in range(width)]
+    for v in range(width):
+        final[v] = resid_ref[v] + ratios[v] * pulled_ref[v]
+    resid = resid_ref[...]
+    told = share_start(links, [resid * resid, final[:width] * image], line, every, (t0, t1))
+    final[width:] = image
+    norm, curve = share_end(told, 2, width, every)
+    seconds = spread(norm / curve, scr0)
+    for v in range(width):
+        final[v] = alphas[v] * pulled_ref[v] + seconds[v] * final[v]
+        final[width + v] = resid_ref[v] - seconds[v] * final[width + v]
     copies = [
         send(final, out_ref.at[links.node], (u0, u1), h - 1, links.on_node(h)) for h in links.node_hops()
     ]
@@ -530,19 +623,12 @@
         cross_body, nodes, ctrs, (out(nodes, 8, owned), out(ctrs, 8, owned)), dma_pair(nodes + ctrs - 2), 2,
         sorted_mine,
     )
-    row_points = row_points.transpose(1, 0, 2).reshape(8, total)[4:]
-    left = row_features(row_points)
+    left, col_right, node_right = factors(row_points, col_points, node_points)
     tiles = owned // LANES
-
-    def tiled(value):
-        shape = (value.shape[0], value.shape[1], tiles, LANES)
-        return value.reshape(shape).transpose(0, 2, 1, 3).reshape(-1, shape[1], LANES)
-
-    col_tiles = tiled(col_points)
-    groups = boxes(row_points, GROUP)
     flat = lambda value: value.transpose(1, 0, 2).reshape(8, -1)[4:]
+    groups = boxes(flat(row_points), GROUP)
     node_lists = near_lists(boxes(flat(node_points), LANES), groups)
-    col_lists = near_lists(boxes(flat(col_tiles), LANES), groups)
+    col_lists = near_lists(boxes(flat(col_points), LANES), groups)
 
     places = jnp.arange(total, dtype=jnp.int32)
     hit = (by_owner.transpose(1, 0, 2).reshape(total) // LANES)[None, :] == (
@@ -557,25 +643,26 @@
     spots = jnp.dot(spots, lane, preferred_element_type=f32).astype(jnp.int32)
     slots = (spots[:tiles] * LANES + spots[tiles:]).reshape(owned)
 
-    part = apply_kernel(node_lists, left, node_points, node_vec, nodes)
-    own_shape, small = out(width, owned), vmem(width, LANES)
-    landing = vmem(nodes - 1, width, owned)
-    every = vmem(devices, width, LANES)
+    own_shape, scr = out(width, tiles, LANES), vmem(width, LANES)
+    cols_shape = out(ctrs, width, tiles, LANES)
+    landing = vmem(nodes - 1, width, tiles, LANES)
+    line, every = vmem(1, LANES), vmem(devices, 1, LANES)
+    part = apply_kernel(node_lists, left, node_right, node_vec, nodes)
     pulled, pulled_cols = comm_call(
-        pulled_body, nodes, ctrs, (own_shape, out(ctrs, width, owned)),
+        pulled_body, nodes, ctrs, (own_shape, cols_shape),
         [landing] + dma_pair(nodes - 1) + dma_pair(ctrs - 1), 3, part,
     )
-    part = apply_kernel(col_lists, left, col_tiles, tiled(pulled_cols), nodes)
+    part = apply_kernel(col_lists, left, col_right, pulled_cols, nodes)
     resid, dir_cols, scal = comm_call(
-        first_body, nodes, ctrs, (own_shape, out(ctrs, width, owned), out(width, LANES)),
-        [landing, vmem(ctrs, width, owned), small, every, small, every]
-        + dma_pair(nodes - 1) + dma_pair(devices - 1) + dma_pair(ctrs - 1) + dma_pair(devices - 1),
+        first_body, nodes, ctrs, (own_shape, cols_shape, out(2, width, LANES)),
+        [landing, vmem(width, tiles, LANES), vmem(ctrs, width, tiles, LANES), line, every, scr, scr]
+        + dma_pair(nodes - 1) + dma_pair(devices - 1) + dma_pair(ctrs - 1),
         4, part, pulled, pulled_cols,
     )
-    part = apply_kernel(col_lists, left, col_tiles, tiled(dir_cols), nodes)
+    part = apply_kernel(col_lists, left, col_right, dir_cols, nodes)
     final = comm_call(
-        second_body, nodes, ctrs, out(nodes, 2 * width, owned),
-        [landing, vmem(2 * width, owned), small, every]
+        second_body, nodes, ctrs, out(nodes, 2 * width, tiles, LANES),
+        [landing, vmem(2 * width, tiles, LANES), line, every, scr]
         + dma_pair(nodes - 1) + dma_pair(devices - 1) + dma_pair(nodes - 1),
         5, part, pulled, resid, scal,
     )

time: 283 us -> 251 us (0.89)
  Pallas kernels: 247 us -> 221 us
  other arithmetic: 23 us -> 18.1 us
    pallas_call x6, Pallas kernels: 133 us -> 104 us  [comm_call(): pl.pallas_call(functools.partial(body, nodes, ctrs), out_shape=out_shape,...]
    unnamed x5 -> x2, other arithmetic: 3.8 us -> 0.01 us
    pallas_call x1 -> x2, Pallas kernels: 12.3 us -> 15.1 us  [the longest x1 12.3 us: node_rows(): pl.pallas_call(node_rows_body, out_shape=[jax.ShapeDtypeStruct((1, 8, cou...]
where the time goes in v2:
time: 251 us; the launch traced here: 248 us
  Pallas kernels  221 us (88%)
  other arithmetic  18.1 us (7%)
  matrix products  4.09 us (2%)
  local copies, waits for them, and re-layouts  2.81 us (1%)
    pallas_call x6, Pallas kernels, comm_call(): pl.pallas_call(functools.partial(body, nodes, ctrs), out_shape=out_shape,...  104 us
    pallas_call x3, Pallas kernels, apply_kernel(): pl.pallas_call(apply_body, out_shape=jax.ShapeDtypeStruct((owners, width,...  99.8 us
    pallas_call x1, Pallas kernels, node_rows(): pl.pallas_call(node_rows_body, out_shape=[jax.ShapeDtypeStruct((1, 8, cou...  12.3 us
    sort x1, other arithmetic, local(): perm = lax.sort(sort_key(plane)) % total  6.77 us
    sort x1, other arithmetic, local(): node_perm = lax.sort(sort_key(volume_xyz)) % volume_xyz.shape[1]  5.78 us

profile of v2, /device:TPU:0, one launch (start us, length us, event | category | flops | bytes accessed | tf_op | source)
XLA Modules:
  0.0 247.6 jit_solution(15757364391766851898)
XLA Ops:
  0.6 0.7 add_select_fusion.12
  1.4 0.8 copy.64
  2.2 16.7 %shard_map.68 = f32[4,8,3,16,128]{4,3,2,1,0:T(8,128)S(1)} custom-call(f32[3,16,128]{2,1,0:T(8,128)S(1)} %bitcast.112), custom_call_target="tpu_custom_call" | custom-call | tf_op jit(solution)/shard_map/pallas_call | solution.py:414
  19.3 0.6 copy.22
  20.0 1.7 select_reduce_fusion.3
  21.7 10.1 %shard_map.69 = f32[8,8,1024]{2,1,0:T(8,128)S(1)} custom-call(f32[8,1024]{1,0:T(8,128)S(1)} %pad.11.own_ref), custom_call_target="tpu_custom_call" | custom-call | tf_op jit(solution)/shard_map/pallas_call | solution.py:414
  32.1 6.8 %sort.28 = (s32[8192]{0:T(1024)S(1)}, s32[8192]{0:T(1024)}) sort(s32[8192]{0:T(1024)S(1)} %fusion.36, s32[8192]{0:T(1024)S(1)} %iota.68), dimensions={0}, to_apply=%region_1.2 | sort | flops 106496 | bytes 131072 | tf_op jit(solution)/shard_map/sort | solution.py:617
  39.1 1.3 fusion.5
  40.5 5.8 %sort.29 = (s32[4096]{0:T(1024)S(1)}, s32[4096]{0:T(1024)}) sort(s32[4096]{0:T(1024)S(1)} %fusion.54, s32[4096]{0:T(1024)S(1)} %iota.72), dimensions={0}, to_apply=%region_10.11 | sort | flops 49152 | bytes 65536 | tf_op jit(solution)/shard_map/sort | solution.py:597
  46.5 12.3 %shard_map.71 = (f32[1,8,4096]{2,1,0:T(8,128)S(1)}, f32[1,12,32,128]{3,2,1,0:T(8,128)S(1)}) custom-call(s32[4096]{0:T(1024)S(1)} %get-tuple-element.69.slab_ref, s32[4096]{0:T(1024)S(1)} %get-tuple-element.68.perm_ref, f32[8,4096]{1,0:T(8,128)S(1)} %maximum_maximum_fusion.xyz_ref, f32[12,4096]{1,0:T(8,128)S(1)} %copy-done), custom_call_target="tpu_custom_call" | custom-call | tf_op jit(solution)/shard_map/pallas_call | solution.py:312
  59.3 0.9 select_reduce_fusion.2
  60.2 9.3 %shard_map.70 = (f32[8,8,1024]{2,1,0:T(8,128)S(1)}, f32[4,8,1024]{2,1,0:T(8,128)S(1)}) custom-call(f32[8,1024]{1,0:T(8,128)S(1)} %maximum_maximum_fusion.1.own_ref), custom_call_target="tpu_custom_call" | custom-call | tf_op jit(solution)/shard_map/pallas_call | solution.py:414
  69.8 0.3 fusion.70
  70.7 1.4 select_reduce_fusion.1
  72.2 2.8 %shard_map.72 = (bf16[8192,128]{1,0:T(8,128)(2,1)S(1)}, bf16[32,128,256]{2,1,0:T(8,128)(2,1)}, bf16[32,128,256]{2,1,0:T(8,128)(2,1)}) custom-call(f32[8,8,1024]{2,1,0:T(8,128)S(1)} %get-tuple-element.20.row_ref, f32[4,8,1024]{2,1,0:T(8,128)S(1)} %get-tuple-element.19.col_ref, f32[1,8,4096]{2,1,0:T(8,128)S(1)} %get-tuple-element.22.node_ref), custom_call_target="tpu_custom_call" | custom-call | tf_op jit(solution)/shard_map/pallas_call | solution.py:263
  75.2 1.4 select_reduce_fusion
  76.7 38.0 %shard_map.73.part_ref = f32[8,12,8,128]{3,2,1,0:T(8,128)S(1)} custom-call(s32[32]{0:T(128)S(1)} %get-tuple-element.40.count, s32[8448]{0:T(1024)S(1)} %pad.13.order, bf16[8192,128]{1,0:T(8,128)(2,1)S(1)} %get-tuple-element.23.left_ref, bf16[32,128,256]{2,1,0:T(8,128)(2,1)} %get-tuple-element.25.right_ref, f32[1,12,32,128]{3,2,1,0:T(8,128)S(1)} %get-tuple-element.26.vec_ref), custom_call_target="tpu_custom_call" | custom-call | tf_op jit(solution)/shard_map/pallas_call | solution.py:204
  114.7 14.4 %shard_map.74 = (f32[12,8,128]{2,1,0:T(8,128)S(1)}, f32[4,12,8,128]{3,2,1,0:T(8,128)S(1)}) custom-call(f32[8,12,8,128]{3,2,1,0:T(8,128)S(1)} %shard_map.73.part_ref), custom_call_target="tpu_custom_call" | custom-call | tf_op jit(solution)/shard_map/pallas_call | solution.py:414
  129.1 30.8 %shard_map.75.part_ref = f32[8,12,8,128]{3,2,1,0:T(8,128)S(1)} custom-call(s32[32]{0:T(128)S(1)} %get-tuple-element.42.count, s32[8448]{0:T(1024)S(1)} %pad.12.order, bf16[8192,128]{1,0:T(8,128)(2,1)S(1)} %get-tuple-element.23.left_ref, bf16[32,128,256]{2,1,0:T(8,128)(2,1)} %get-tuple-element.24.right_ref, ...), custom_call_target="tpu_custom_call" | custom-call | tf_op jit(solution)/shard_map/pallas_call | solution.py:204
  159.9 21.2 %shard_map.76 = (f32[12,8,128]{2,1,0:T(8,128)S(1)}, f32[4,12,8,128]{3,2,1,0:T(8,128)S(1)}, f32[2,12,128]{2,1,0:T(8,128)S(1)}) custom-call(f32[8,12,8,128]{3,2,1,0:T(8,128)S(1)} %shard_map.75.part_ref, f32[12,8,128]{2,1,0:T(8,128)S(1)} %get-tuple-element.28.pulled_ref, f32[4,12,8,128]{3,2,1,0:T(8,128)S(1)} %get-tuple-element.27.vec_ref.pulled_cols), custom_call_target="tpu_custom_call" | custom-call | tf_op jit(solution)/shard_map/pallas_call | solution.py:414
  181.2 31.0 %shard_map.77.part_ref = f32[8,12,8,128]{3,2,1,0:T(8,128)S(1)} custom-call(s32[32]{0:T(128)S(1)} %get-tuple-element.42.count, s32[8448]{0:T(1024)S(1)} %pad.12.order, bf16[8192,128]{1,0:T(8,128)(2,1)S(1)} %get-tuple-element.23.left_ref, bf16[32,128,256]{2,1,0:T(8,128)(2,1)} %get-tuple-element.24.right_ref, f32[4,12,8,128]{3,2,1,0:T(8,128)S(1)} %get-tuple-element.29.vec_ref), custom_call_target="tpu_custom_call" | custom-call | tf_op jit(solution)/shard_map/pallas_call | solution.py:204
  212.2 31.7 %shard_map.78.table_ref = f32[8,24,8,128]{3,2,1,0:T(8,128)S(1)} custom-call(f32[8,12,8,128]{3,2,1,0:T(8,128)S(1)} %shard_map.77.part_ref, f32[12,8,128]{2,1,0:T(8,128)S(1)} %get-tuple-element.28.pulled_ref, f32[12,8,128]{2,1,0:T(8,128)S(1)} %get-tuple-element.30.resid_ref, f32[2,12,128]{2,1,0:T(8,128)S(1)} %get-tuple-element.31.scal_ref), custom_call_target="tpu_custom_call" | custom-call | tf_op jit(solution)/shard_map/pallas_call | solution.py:414
  243.9 3.0 %shard_map.79 = f32[24,1024]{1,0:T(8,128)S(1)} custom-call(s32[1024]{0:T(1024)S(1)} %fusion.64.slot_ref, f32[8,24,8,128]{3,2,1,0:T(8,128)S(1)} %shard_map.78.table_ref), custom_call_target="tpu_custom_call" | custom-call | tf_op jit(solution)/shard_map/pallas_call | solution.py:347
  246.9 0.7 fusion.72
  (63 shorter events, 2.8 us)
Async XLA Ops:
  21.6 18.8 %copy-start.1 = (f32[3,4096]{1,0:T(4,128)S(1)}, f32[3,4096]{1,0:T(4,128)}, u32[]{:S(2)}) copy-start(f32[3,4096]{1,0:T(4,128)} %param.7) | copy-start | bytes 147460
  21.6 24.7 %copy-start.2 = (s32[4096]{0:T(1024)S(1)}, s32[4096]{0:T(1024)}, u32[]{:S(2)}) copy-start(s32[4096]{0:T(1024)} %param.8) | copy-start | bytes 49156
  21.7 24.9 %copy-start = (f32[12,4096]{1,0:T(8,128)S(1)}, f32[12,4096]{1,0:T(8,128)}, u32[]{:S(2)}) copy-start(f32[12,4096]{1,0:T(8,128)} %cot_ref.1) | copy-start | bytes 589828

commit v3 on v2

--- a/solution.py
+++ b/solution.py
@@ -89,14 +89,16 @@
     return jnp.min(tiles, axis=2), jnp.max(tiles, axis=2)
 
 
-def near_lists(tiles, groups):
+def near_lists(tiles, groups, pieces):
     gap = jnp.maximum(
         jnp.maximum(tiles[0][:, :, None] - groups[1][:, None, :], groups[0][:, None, :] - tiles[1][:, :, None]),
         0.0,
     )
     near = jnp.sum(gap * gap, axis=0) < 1.0 + 1e-4
+    size = near.shape[1]
+    near = jnp.any(near.reshape(-1, pieces, size), axis=1)
+    total = near.shape[0]
     count = jnp.sum(near.astype(jnp.int32), axis=1)
-    size = near.shape[1]
     upto = (jnp.arange(size)[:, None] <= jnp.arange(size)[None, :]).astype(jnp.bfloat16)
     seen = jnp.dot(near.astype(jnp.bfloat16), upto, preferred_element_type=jnp.float32).astype(jnp.int32)
     every = jnp.arange(size, dtype=jnp.int32)
@@ -104,10 +106,19 @@
     order = jnp.sum(
         jnp.where(place[:, :, None] == every[None, None, :], every[None, :, None], 0), axis=1
     )
-    return count, jnp.pad((order * GROUP).reshape(-1), (0, size))
-
-
-def apply_body(count, order, left_ref, right_ref, vec_ref, out_ref, acc, vec, items, q0, q1, k0, k1):
+    batches = (count + BATCH - 1) // BATCH
+    ranks = jnp.arange(total)
+    ends = jnp.sum(jnp.where(ranks[:, None] <= ranks[None, :], batches[:, None], 0), axis=0)
+    at = jnp.arange(total * size // BATCH + 8 * PAIR, dtype=jnp.int32) - 2 * PAIR
+    passed = ends[:, None] <= at[None, :]
+    tile = jnp.sum(passed.astype(jnp.int32), axis=0)
+    start = jnp.sum(jnp.where(passed, batches[:, None], 0), axis=0)
+    code = tile * size + (at - start) * BATCH
+    items = jnp.where((at < 0) | (tile == total), total * size, code)
+    return ends[-1:], items, jnp.pad((order * GROUP).reshape(-1), (0, size))
+
+
+def apply_body(count, items, order, left_ref, right_ref, vec_ref, out_ref, acc, vec, q0, q1, k0, k1):
     rows = left_ref.shape[0]
     tiles = right_ref.shape[0]
     span = GROUP * BATCH
@@ -125,21 +136,6 @@
     vec[tiles] = jnp.zeros_like(vec[tiles])
 
     groups = rows // GROUP
-    nothing = tiles * groups
-    for index in range(2 * PAIR):
-        items[index] = nothing
-
-    def fill(tile, at):
-        def one(batch, at):
-            items[at] = tile * groups + batch * BATCH
-            return at + 1
-
-        return lax.fori_loop(0, (count[tile] + BATCH - 1) // BATCH, one, at)
-
-    end = lax.fori_loop(0, tiles, fill, 2 * PAIR)
-    for index in range(4 * PAIR):
-        items[end + index] = nothing
-
     first_half = lax.broadcasted_iota(jnp.int32, (half, LANES), 1) < LANES // 2
 
     def item(index):
@@ -185,7 +181,7 @@
         step(2 * index + 1, q1, q0, k1, k0)
         return 0
 
-    steps = (end - 2 * PAIR + PAIR - 1) // PAIR + 2
+    steps = (count[0] + PAIR - 1) // PAIR + 2
     lax.fori_loop(0, (steps + 1) // 2, two_steps, 0)
 
     owners, _, high, _ = out_ref.shape
@@ -196,7 +192,6 @@
 
 
 def apply_kernel(lists, left, right, vec, owners):
-    count, order = lists
     rows = left.shape[0]
     tiles = right.shape[0]
     width = vec.shape[1]
@@ -204,19 +199,18 @@
     return pl.pallas_call(
         apply_body,
         out_shape=jax.ShapeDtypeStruct((owners, width, rows // owners // LANES, LANES), jnp.float32),
-        in_specs=[pl.BlockSpec(memory_space=pltpu.SMEM)] * 2 + [pl.BlockSpec(memory_space=pltpu.VMEM)] * 3,
+        in_specs=[pl.BlockSpec(memory_space=pltpu.SMEM)] * 3 + [pl.BlockSpec(memory_space=pltpu.VMEM)] * 3,
         out_specs=pl.BlockSpec(memory_space=pltpu.VMEM),
         scratch_shapes=[
             pltpu.VMEM((rows, 2 * PAD), jnp.float32),
             pltpu.VMEM((tiles + 1, 2 * PAD, 2 * LANES), jnp.bfloat16),
-            pltpu.SMEM((tiles * (rows // (GROUP * BATCH)) + 8 * PAIR,), jnp.int32),
             pltpu.VMEM((wide // 2, 2 * LANES), jnp.float32),
             pltpu.VMEM((wide // 2, 2 * LANES), jnp.float32),
             pltpu.VMEM((wide, 2 * LANES), jnp.bfloat16),
             pltpu.VMEM((wide, 2 * LANES), jnp.bfloat16),
         ],
         compiler_params=pltpu.CompilerParams(vmem_limit_bytes=VMEM),
-    )(count, order, left, right, vec)
+    )(*lists, left, right, vec)
 
 
 def factor_body(row_ref, col_ref, node_ref, left_ref, col_out, node_out):
@@ -282,23 +276,23 @@
         rows_a[here, :PAD] = jnp.concatenate([cot_ref[:, here], blank], axis=0).T
 
     def scatter(index, _):
-        base = pl.multiple_of(index * 16, 16)
-        for i in range(16):
+        base = pl.multiple_of(index * 64, 64)
+        for i in range(64):
             rows_b[pl.ds(slab_ref[base + i], 1), :] = rows_a[pl.ds(base + i, 1), :]
         return 0
 
-    lax.fori_loop(0, count // 16, scatter, 0)
+    lax.fori_loop(0, count // 64, scatter, 0)
     for tile in range(count // LANES):
         here = pl.ds(tile * LANES, LANES)
         rows_b[here, PAD : PAD + 8] = xyz_ref[:, here].T
 
     def gather(index, _):
-        base = pl.multiple_of(index * 16, 16)
-        for i in range(16):
+        base = pl.multiple_of(index * 64, 64)
+        for i in range(64):
             rows_c[pl.ds(base + i, 1), :] = rows_b[pl.ds(perm_ref[base + i], 1), :]
         return 0
 
-    lax.fori_loop(0, count // 16, gather, 0)
+    lax.fori_loop(0, count // 64, gather, 0)
     for tile in range(count // LANES):
         here = rows_c[pl.ds(tile * LANES, LANES), :].T
         cot_out[0, :, tile, :] = here[:width]
@@ -330,12 +324,12 @@
             rows_a[pl.ds((block * deep + tile) * LANES, LANES), :width] = table_ref[block, :, tile, :].T
 
     def gather(index, _):
-        base = pl.multiple_of(index * 16, 16)
-        for i in range(16):
+        base = pl.multiple_of(index * 64, 64)
+        for i in range(64):
             rows_b[pl.ds(base + i, 1), :] = rows_a[pl.ds(slot_ref[base + i], 1), :]
         return 0
 
-    lax.fori_loop(0, count // 16, gather, 0)
+    lax.fori_loop(0, count // 64, gather, 0)
     for tile in range(count // LANES):
         here = pl.ds(tile * LANES, LANES)
         out_ref[:, here] = rows_b[here, :].T[:width]
@@ -627,8 +621,8 @@
     tiles = owned // LANES
     flat = lambda value: value.transpose(1, 0, 2).reshape(8, -1)[4:]
     groups = boxes(flat(row_points), GROUP)
-    node_lists = near_lists(boxes(flat(node_points), LANES), groups)
-    col_lists = near_lists(boxes(flat(col_points), LANES), groups)
+    node_lists = near_lists(boxes(flat(node_points), LANES // 2), groups, 2)
+    col_lists = near_lists(boxes(flat(col_points), LANES), groups, 1)
 
     places = jnp.arange(total, dtype=jnp.int32)
     hit = (by_owner.transpose(1, 0, 2).reshape(total) // LANES)[None, :] == (

time: 251 us -> 246 us (0.980)
  Pallas kernels: 221 us -> 215 us
    pallas_call x3, Pallas kernels: 99.8 us -> 92.8 us  [apply_kernel(): pl.pallas_call(apply_body, out_shape=jax.ShapeDtypeStruct((owners, width,...]
where the time goes in v3:
time: 246 us; the launch traced here: 243 us
  Pallas kernels  215 us (87%)
  other arithmetic  18.7 us (8%)
  local copies, waits for them, and re-layouts  4.12 us (2%)
  matrix products  4.09 us (2%)
    pallas_call x6, Pallas kernels, comm_call(): pl.pallas_call(functools.partial(body, nodes, ctrs), out_shape=out_shape,...  106 us
    pallas_call x3, Pallas kernels, apply_kernel(): pl.pallas_call(apply_body, out_shape=jax.ShapeDtypeStruct((owners, width,...  92.8 us
    pallas_call x1, Pallas kernels, node_rows(): pl.pallas_call(node_rows_body, out_shape=[jax.ShapeDtypeStruct((1, 8, cou...  10.6 us
    sort x1, other arithmetic, local(): perm = lax.sort(sort_key(plane)) % total  6.77 us
    sort x1, other arithmetic, local(): node_perm = lax.sort(sort_key(volume_xyz)) % volume_xyz.shape[1]  5.78 us

profile of v3, /device:TPU:0, one launch (start us, length us, event | category | flops | bytes accessed | tf_op | source)
XLA Modules:
  0.0 243.1 jit_solution(716764111120953262)
XLA Ops:
  0.6 0.7 add_select_fusion.14
  1.4 0.8 copy.61
  2.2 16.7 %shard_map.68 = f32[4,8,3,16,128]{4,3,2,1,0:T(8,128)S(1)} custom-call(f32[3,16,128]{2,1,0:T(8,128)S(1)} %bitcast.106), custom_call_target="tpu_custom_call" | custom-call | tf_op jit(solution)/shard_map/pallas_call | solution.py:408
  19.3 0.6 copy.22
  20.0 1.7 select_reduce_fusion.3
  21.7 10.1 %shard_map.69 = f32[8,8,1024]{2,1,0:T(8,128)S(1)} custom-call(f32[8,1024]{1,0:T(8,128)S(1)} %pad.11.own_ref), custom_call_target="tpu_custom_call" | custom-call | tf_op jit(solution)/shard_map/pallas_call | solution.py:408
  32.1 6.8 %sort.28 = (s32[8192]{0:T(1024)S(1)}, s32[8192]{0:T(1024)}) sort(s32[8192]{0:T(1024)S(1)} %fusion.40, s32[8192]{0:T(1024)S(1)} %iota.92), dimensions={0}, to_apply=%region_1.2 | sort | flops 106496 | bytes 131072 | tf_op jit(solution)/shard_map/sort | solution.py:611
  39.1 1.3 fusion.5
  40.6 0.9 select_reduce_fusion.2
  41.7 9.3 %shard_map.70 = (f32[8,8,1024]{2,1,0:T(8,128)S(1)}, f32[4,8,1024]{2,1,0:T(8,128)S(1)}) custom-call(f32[8,1024]{1,0:T(8,128)S(1)} %maximum_maximum_fusion.1.own_ref), custom_call_target="tpu_custom_call" | custom-call | tf_op jit(solution)/shard_map/pallas_call | solution.py:408
  52.1 0.6 slice.107.count
  52.8 5.8 %sort.29 = (s32[4096]{0:T(1024)S(1)}, s32[4096]{0:T(1024)}) sort(s32[4096]{0:T(1024)S(1)} %fusion.58, s32[4096]{0:T(1024)S(1)} %iota.97), dimensions={0}, to_apply=%region_13.14 | sort | flops 49152 | bytes 65536 | tf_op jit(solution)/shard_map/sort | solution.py:591
  58.7 10.6 %shard_map.71 = (f32[1,8,4096]{2,1,0:T(8,128)S(1)}, f32[1,12,32,128]{3,2,1,0:T(8,128)S(1)}) custom-call(s32[4096]{0:T(1024)S(1)} %get-tuple-element.71.slab_ref, s32[4096]{0:T(1024)S(1)} %get-tuple-element.70.perm_ref, f32[8,4096]{1,0:T(8,128)S(1)} %maximum_maximum_fusion.xyz_ref, f32[12,4096]{1,0:T(8,128)S(1)} %copy-done), custom_call_target="tpu_custom_call" | custom-call | tf_op jit(solution)/shard_map/pallas_call | solution.py:306
  70.5 1.4 select_reduce_fusion.1
  72.0 2.8 %shard_map.72 = (bf16[8192,128]{1,0:T(8,128)(2,1)S(1)}, bf16[32,128,256]{2,1,0:T(8,128)(2,1)}, bf16[32,128,256]{2,1,0:T(8,128)(2,1)}) custom-call(f32[8,8,1024]{2,1,0:T(8,128)S(1)} %get-tuple-element.20.row_ref, f32[4,8,1024]{2,1,0:T(8,128)S(1)} %get-tuple-element.19.col_ref, f32[1,8,4096]{2,1,0:T(8,128)S(1)} %get-tuple-element.22.node_ref), custom_call_target="tpu_custom_call" | custom-call | tf_op jit(solution)/shard_map/pallas_call | solution.py:257
  75.5 1.4 select_reduce_fusion
  76.9 35.1 %shard_map.73.part_ref = f32[8,12,8,128]{3,2,1,0:T(8,128)S(1)} custom-call(s32[1]{0:T(128)} %slice.113.count, s32[1040]{0:T(1024)S(1)} %add_select_fusion.10.items, s32[8448]{0:T(1024)S(1)} %pad.13.order, bf16[8192,128]{1,0:T(8,128)(2,1)S(1)} %get-tuple-element.23.left_ref, bf16[32,128,256]{2,1,0:T(8,128)(2,1)} %get-tuple-element.25.right_ref, ...), custom_call_target="tpu_custom_call" | custom-call | tf_op jit(solution)/shard_map/pallas_call | solution.py:199
  112.1 16.5 %shard_map.74 = (f32[12,8,128]{2,1,0:T(8,128)S(1)}, f32[4,12,8,128]{3,2,1,0:T(8,128)S(1)}) custom-call(f32[8,12,8,128]{3,2,1,0:T(8,128)S(1)} %shard_map.73.part_ref), custom_call_target="tpu_custom_call" | custom-call | tf_op jit(solution)/shard_map/pallas_call | solution.py:408
  128.6 28.8 %shard_map.75.part_ref = f32[8,12,8,128]{3,2,1,0:T(8,128)S(1)} custom-call(s32[1]{0:T(128)} %slice.107.count, s32[1040]{0:T(1024)S(1)} %add_select_fusion.11.items, s32[8448]{0:T(1024)S(1)} %pad.12.order, bf16[8192,128]{1,0:T(8,128)(2,1)S(1)} %get-tuple-element.23.left_ref, bf16[32,128,256]{2,1,0:T(8,128)(2,1)} %get-tuple-element.24.right_ref, ...), custom_call_target="tpu_custom_call" | custom-call | tf_op jit(solution)/shard_map/pallas_call | solution.py:199
  157.4 21.6 %shard_map.76 = (f32[12,8,128]{2,1,0:T(8,128)S(1)}, f32[4,12,8,128]{3,2,1,0:T(8,128)S(1)}, f32[2,12,128]{2,1,0:T(8,128)S(1)}) custom-call(f32[8,12,8,128]{3,2,1,0:T(8,128)S(1)} %shard_map.75.part_ref, f32[12,8,128]{2,1,0:T(8,128)S(1)} %get-tuple-element.28.pulled_ref, f32[4,12,8,128]{3,2,1,0:T(8,128)S(1)} %get-tuple-element.27.vec_ref.pulled_cols), custom_call_target="tpu_custom_call" | custom-call | tf_op jit(solution)/shard_map/pallas_call | solution.py:408
  179.0 28.8 %shard_map.77.part_ref = f32[8,12,8,128]{3,2,1,0:T(8,128)S(1)} custom-call(s32[1]{0:T(128)} %slice.107.count, s32[1040]{0:T(1024)S(1)} %add_select_fusion.11.items, s32[8448]{0:T(1024)S(1)} %pad.12.order, bf16[8192,128]{1,0:T(8,128)(2,1)S(1)} %get-tuple-element.23.left_ref, bf16[32,128,256]{2,1,0:T(8,128)(2,1)} %get-tuple-element.24.right_ref, ...), custom_call_target="tpu_custom_call" | custom-call | tf_op jit(solution)/shard_map/pallas_call | solution.py:199
  207.9 31.7 %shard_map.78.table_ref = f32[8,24,8,128]{3,2,1,0:T(8,128)S(1)} custom-call(f32[8,12,8,128]{3,2,1,0:T(8,128)S(1)} %shard_map.77.part_ref, f32[12,8,128]{2,1,0:T(8,128)S(1)} %get-tuple-element.28.pulled_ref, f32[12,8,128]{2,1,0:T(8,128)S(1)} %get-tuple-element.30.resid_ref, f32[2,12,128]{2,1,0:T(8,128)S(1)} %get-tuple-element.31.scal_ref), custom_call_target="tpu_custom_call" | custom-call | tf_op jit(solution)/shard_map/pallas_call | solution.py:408
  239.6 2.8 %shard_map.79 = f32[24,1024]{1,0:T(8,128)S(1)} custom-call(s32[1024]{0:T(1024)S(1)} %fusion.71.slot_ref, f32[8,24,8,128]{3,2,1,0:T(8,128)S(1)} %shard_map.78.table_ref), custom_call_target="tpu_custom_call" | custom-call | tf_op jit(solution)/shard_map/pallas_call | solution.py:341
  242.4 0.7 fusion.80
  (78 shorter events, 4.5 us)
Async XLA Ops:
  40.6 12.1 %copy-start.1 = (f32[3,4096]{1,0:T(4,128)S(1)}, f32[3,4096]{1,0:T(4,128)}, u32[]{:S(2)}) copy-start(f32[3,4096]{1,0:T(4,128)} %param.7) | copy-start | bytes 147460
  41.5 17.1 %copy-start.2 = (s32[4096]{0:T(1024)S(1)}, s32[4096]{0:T(1024)}, u32[]{:S(2)}) copy-start(s32[4096]{0:T(1024)} %param.8) | copy-start | bytes 49156
  41.5 17.2 %copy-start = (f32[12,4096]{1,0:T(8,128)S(1)}, f32[12,4096]{1,0:T(8,128)}, u32[]{:S(2)}) copy-start(f32[12,4096]{1,0:T(8,128)} %cot_ref.1) | copy-start | bytes 589828

commit v4 on v3

--- a/solution.py
+++ b/solution.py
@@ -11,8 +11,8 @@
 RADIUS = 0.2
 LANES = 128
 GROUP = 32
-BATCH = 8
-PAIR = 2
+BATCH = 4
+PAIR = 4
 CELLS = 5
 DEPTH = 64
 PAD = 16
@@ -21,37 +21,9 @@
 MESH = pl.DeviceIdType.MESH
 
 
-def split3(value):
-    first = lax.reduce_precision(value, 8, 7)
-    rest = value - first
-    second = lax.reduce_precision(rest, 8, 7)
-    return first, second, lax.reduce_precision(rest - second, 8, 7)
-
-
-def lookup(table, ids):
-    rows = table.shape[1] // LANES
-    parts = jnp.concatenate([part.reshape(3, rows, LANES) for part in split3(table)], axis=0)
-    parts = parts.transpose(1, 0, 2).reshape(rows, 9 * LANES).astype(jnp.bfloat16)
-    high = (ids[:, None] // LANES == jnp.arange(rows, dtype=jnp.int32)[None, :]).astype(jnp.bfloat16)
-    picked = jnp.dot(high, parts, preferred_element_type=jnp.float32)
-    low = ids[:, None] % LANES == jnp.arange(LANES, dtype=jnp.int32)[None, :]
-    picked = picked.reshape(-1, 9, LANES)
-    picked = jnp.sum(jnp.where(low[:, None, :], picked, 0.0), axis=2)
-    return (picked[:, 0:3] + picked[:, 3:6] + picked[:, 6:9]).T
-
-
 def scaled(xyz):
     point = (xyz - 0.5) * (1.0 / RADIUS)
     return jnp.concatenate([point, jnp.ones((1, xyz.shape[1]), jnp.float32)], axis=0)
-
-
-def row_features(point):
-    square = jnp.sum(point[:3] * point[:3], axis=0, keepdims=True)
-    alpha = jnp.concatenate(
-        [jnp.ones_like(square), jnp.zeros_like(point[:3]), -2.0 * point[:3], square], axis=0
-    )
-    a1, a2, a3 = split3(alpha)
-    return jnp.concatenate([a1, a1, a2, a2, a1, a3], axis=0).T.astype(jnp.bfloat16)
 
 
 def rounded(value):
@@ -73,15 +45,6 @@
 def two_parts(vectors):
     v1 = rounded(vectors)
     return jnp.concatenate([v1, vectors - v1], axis=0).astype(jnp.bfloat16)
-
-
-def sort_key(xyz):
-    count = xyz.shape[1]
-    cell = jnp.minimum((xyz[:2] * CELLS).astype(jnp.int32), CELLS - 1)
-    deep = jnp.minimum((xyz[2] * DEPTH).astype(jnp.int32), DEPTH - 1)
-    column = cell[0] * CELLS + jnp.where(cell[0] % 2 == 1, CELLS - 1 - cell[1], cell[1])
-    deep = jnp.where(column % 2 == 1, DEPTH - 1 - deep, deep)
-    return (column * DEPTH + deep) * count + jnp.arange(count, dtype=jnp.int32)
 
 
 def boxes(points, size):
@@ -421,45 +384,117 @@
     return [pltpu.SemaphoreType.DMA((count,))] * 2
 
 
-def surface_body(nodes, ctrs, own_ref, all_ref, *sems):
+TN = (((0,), (0,)), ((), ()))
+
+
+def picked(tables, rows, lanes):
+    high = lax.broadcasted_iota(jnp.int32, (tables[0].shape[0], rows.shape[1]), 0) == rows
+    high = jnp.where(high, 1.0, 0.0).astype(jnp.bfloat16)
+    low = lax.broadcasted_iota(jnp.int32, (LANES, rows.shape[1]), 0) == lanes
+    found = []
+    for table in tables:
+        a1 = rounded(table)
+        a2 = rounded(table - a1)
+        a3 = table - a1 - a2
+        parts = jnp.concatenate([a1, a2, a3], axis=1).astype(jnp.bfloat16)
+        both = lax.dot_general(parts, high, TN, preferred_element_type=jnp.float32)
+        value = both[:LANES] + both[LANES : 2 * LANES] + both[2 * LANES :]
+        found.append(jnp.sum(jnp.where(low, value, 0.0), axis=0, keepdims=True))
+    return found
+
+
+def cell_keys(x, y, z):
+    rows = x.shape[0]
+    count = rows * LANES
+    across = jnp.minimum((x * CELLS).astype(jnp.int32), CELLS - 1)
+    along = jnp.minimum((y * CELLS).astype(jnp.int32), CELLS - 1)
+    deep = jnp.minimum((z * DEPTH).astype(jnp.int32), DEPTH - 1)
+    column = across * CELLS + jnp.where(across % 2 == 1, CELLS - 1 - along, along)
+    deep = jnp.where(column % 2 == 1, DEPTH - 1 - deep, deep)
+    index = lax.broadcasted_iota(jnp.int32, x.shape, 0) * LANES + lax.broadcasted_iota(jnp.int32, x.shape, 1)
+    return ((column * DEPTH + deep) * count + index).astype(jnp.float32)
+
+
+def sorted_keys(keys):
+    rows = keys.shape[0]
+    row = lax.broadcasted_iota(jnp.int32, keys.shape, 0)
+    lane = lax.broadcasted_iota(jnp.int32, keys.shape, 1)
+    bits = (rows * LANES).bit_length() - 1
+
+    def bit(at):
+        return (lane // 2**at) % 2 == 0 if at < 7 else (row // 2 ** (at - 7)) % 2 == 0
+
+    zeros = [bit(at) for at in range(bits)]
+    for level in range(1, bits + 1):
+        for at in range(level - 1, -1, -1):
+            axis, size, shift = (1, LANES, 2**at) if at < 7 else (0, rows, 2 ** (at - 7))
+            other = jnp.where(
+                zeros[at], pltpu.roll(keys, size - shift, axis), pltpu.roll(keys, shift, axis)
+            )
+            small = zeros[at] if level == bits else zeros[at] == zeros[level]
+            keys = jnp.where(small, jnp.minimum(keys, other), jnp.maximum(keys, other))
+    return keys
+
+
+def setup_body(
+    nodes, ctrs, own_ref, ids_ref, volume_ref, perm_ref, node_ref, ctr_ref, slab_ref,
+    all_ref, mine_ref, plane_ref, table_ref, point_ref, *sems,
+):
     links = Links(nodes, ctrs)
     links.meet_sides()
     mine = all_ref.at[links.ctr, links.node]
-    copies = [send(own_ref, mine, sems, h - 1, links.on_node(h)) for h in links.node_hops()]
+    copies = [send(own_ref, mine, sems[:2], h - 1, links.on_node(h)) for h in links.node_hops()]
     all_ref[links.ctr, links.node] = own_ref[...]
+    keys = sorted_keys(cell_keys(*(volume_ref[k] for k in range(3))))
+    slab_ref[...] = keys.astype(jnp.int32) % (keys.shape[0] * LANES)
     finish(copies)
     whole = all_ref.at[links.ctr]
     last = nodes - 1
-    if ctrs != 4:
-        finish([send(whole, whole, sems, last - 1 + h, links.on_ctr(h)) for h in links.ctr_hops()])
-        return
-    far = lax.rem(links.ctr + 2, 4)
-    near = (links.node, links.ctr + 1 - 2 * lax.rem(links.ctr, 2))
-    across = send(whole, whole, sems, last, (links.node, far))
-    beside = send(whole, whole, sems, last + 1, near)
-    across.wait()
-    other = all_ref.at[far]
-    finish([send(other, other, sems, last + 2, near), beside])
-
-
-def node_body(nodes, ctrs, own_ref, all_ref, *sems):
-    links = Links(nodes, ctrs)
-    links.meet([links.on_node(h) for h in links.node_hops()])
-    mine = all_ref.at[links.node]
-    copies = [send(own_ref, mine, sems, h - 1, links.on_node(h)) for h in links.node_hops()]
-    all_ref[links.node] = own_ref[...]
+    if ctrs == 4:
+        far = lax.rem(links.ctr + 2, 4)
+        near = (links.node, links.ctr + 1 - 2 * lax.rem(links.ctr, 2))
+        across = send(whole, whole, sems[:2], last, (links.node, far))
+        beside = send(whole, whole, sems[:2], last + 1, near)
+        across.wait()
+        other = all_ref.at[far]
+        finish([send(other, other, sems[:2], last + 2, near), beside])
+    else:
+        finish([send(whole, whole, sems[:2], last - 1 + h, links.on_ctr(h)) for h in links.ctr_hops()])
+
+    rows, tiles = own_ref.shape[1], mine_ref.shape[1]
+    tables = [all_ref[:, :, k].reshape(-1, LANES) for k in range(3)]
+    for at in range(tiles):
+        ids = ids_ref[at : at + 1, :]
+        device = ids // (rows * LANES)
+        place = (device % ctrs * nodes + device // ctrs) * rows + ids // LANES % rows
+        for k, value in enumerate(picked(tables, place, ids % LANES)):
+            mine_ref[k, at : at + 1, :] = value
+    copies = [
+        send(mine_ref, plane_ref.at[links.node], sems[2:4], h - 1, links.on_node(h)) for h in links.node_hops()
+    ]
+    plane_ref[links.node] = mine_ref[...]
     finish(copies)
 
-
-def cross_body(nodes, ctrs, own_ref, node_ref, ctr_ref, *sems):
-    links = Links(nodes, ctrs)
-    links.meet_sides()
-    copies = [send(own_ref, node_ref.at[links.node], sems, h - 1, links.on_node(h)) for h in links.node_hops()]
+    for node in range(nodes):
+        for k in range(3):
+            table_ref[k, node * tiles : (node + 1) * tiles, :] = plane_ref[node, k]
+    tables = [table_ref[k] for k in range(3)]
+    count = tables[0].shape[0] * LANES
+    keys = sorted_keys(cell_keys(*tables))
+    perm_ref[...] = keys.astype(jnp.int32) % count
+    blank = jnp.zeros((4, LANES), jnp.float32)
+    for at in range(tiles):
+        ids = perm_ref[pl.ds(at * nodes + links.node, 1), :]
+        found = [(v - 0.5) * (1.0 / RADIUS) for v in picked(tables, ids // LANES, ids % LANES)]
+        point_ref[:, at * LANES : (at + 1) * LANES] = jnp.concatenate(
+            [blank] + found + [jnp.ones((1, LANES), jnp.float32)], axis=0
+        )
+    copies = [send(point_ref, node_ref.at[links.node], sems[4:6], h - 1, links.on_node(h)) for h in links.node_hops()]
     copies += [
-        send(own_ref, ctr_ref.at[links.ctr], sems, nodes - 2 + h, links.on_ctr(h)) for h in links.ctr_hops()
+        send(point_ref, ctr_ref.at[links.ctr], sems[4:6], nodes - 2 + h, links.on_ctr(h)) for h in links.ctr_hops()
     ]
-    node_ref[links.node] = own_ref[...]
-    ctr_ref[links.ctr] = own_ref[...]
+    node_ref[links.node] = point_ref[...]
+    ctr_ref[links.ctr] = point_ref[...]
     finish(copies)
 
 
@@ -588,37 +623,29 @@
     devices = nodes * ctrs
 
     slab = slab_ids % volume_xyz.shape[1]
-    node_perm = lax.sort(sort_key(volume_xyz)) % volume_xyz.shape[1]
     volume_points = jnp.concatenate(
         [scaled(volume_xyz), jnp.zeros((4, volume_xyz.shape[1]), f32)], axis=0
     )
     volume_points = jnp.concatenate([volume_points[4:], volume_points[:4]], axis=0)
-    node_points, node_vec = node_rows(slab, node_perm, volume_points, cotangent)
 
     rows = surface_xyz.shape[1] // LANES
-    surface = comm_call(
-        surface_body, nodes, ctrs, out(ctrs, nodes, 3, rows, LANES), dma_pair(nodes + ctrs - 2), 0,
-        surface_xyz.reshape(3, rows, LANES),
-    )
-    surface = surface.transpose(2, 1, 0, 3, 4).reshape(3, -1)
-    mine = lookup(surface, centre_idx)
-
-    plane = comm_call(
-        node_body, nodes, ctrs, out(nodes, 8, owned), dma_pair(nodes - 1), 1,
-        jnp.pad(mine, ((0, 5), (0, 0))),
-    )[:, :3]
-    plane = plane.transpose(1, 0, 2).reshape(3, total)
-    perm = lax.sort(sort_key(plane)) % total
-    by_owner = perm.reshape(owned // LANES, nodes, LANES)
-    own_perm = lax.dynamic_index_in_dim(by_owner, here, 1, False).reshape(owned)
-    sorted_mine = scaled(lookup(plane, own_perm))
-    sorted_mine = jnp.concatenate([jnp.zeros_like(sorted_mine), sorted_mine], axis=0)
-    row_points, col_points = comm_call(
-        cross_body, nodes, ctrs, (out(nodes, 8, owned), out(ctrs, 8, owned)), dma_pair(nodes + ctrs - 2), 2,
-        sorted_mine,
-    )
+    tiles = owned // LANES
+    perm, row_points, col_points, node_perm = comm_call(
+        setup_body, nodes, ctrs,
+        (
+            jax.ShapeDtypeStruct((total // LANES, LANES), jnp.int32), out(nodes, 8, owned), out(ctrs, 8, owned),
+            jax.ShapeDtypeStruct((volume_xyz.shape[1] // LANES, LANES), jnp.int32),
+        ),
+        [
+            vmem(ctrs, nodes, 3, rows, LANES), vmem(3, tiles, LANES), vmem(nodes, 3, tiles, LANES),
+            vmem(3, total // LANES, LANES), vmem(8, owned),
+        ] + dma_pair(nodes + ctrs - 2) + dma_pair(nodes - 1) + dma_pair(nodes + ctrs - 2),
+        0, surface_xyz.reshape(3, rows, LANES), centre_idx.reshape(tiles, LANES),
+        volume_xyz.reshape(3, -1, LANES),
+    )
+    by_owner = perm.reshape(tiles, nodes, LANES)
+    node_points, node_vec = node_rows(slab, node_perm.reshape(-1), volume_points, cotangent)
     left, col_right, node_right = factors(row_points, col_points, node_points)
-    tiles = owned // LANES
     flat = lambda value: value.transpose(1, 0, 2).reshape(8, -1)[4:]
     groups = boxes(flat(row_points), GROUP)
     node_lists = near_lists(boxes(flat(node_points), LANES // 2), groups, 2)

time: 246 us -> 227 us (0.923)
  other arithmetic: 18.7 us -> 4.65 us
  Pallas kernels: 215 us -> 211 us
  matrix products: 4.09 us -> 1.57 us
    sort x2 -> x0, other arithmetic: 12.5 us -> none  [the longest x1 6.77 us: local(): perm = lax.sort(sort_key(plane)) % total]
    pallas_call x3, Pallas kernels: 92.8 us -> 88.1 us  [apply_kernel(): pl.pallas_call(apply_body, out_shape=jax.ShapeDtypeStruct((owners, width,...]
    dot_general x2 -> x0, matrix products: 2.52 us -> none  [lookup(): picked = jnp.dot(high, parts, preferred_element_type=jnp.float32)]
    pallas_call x6 -> x4, Pallas kernels: 106 us -> 107 us  [comm_call(): pl.pallas_call(functools.partial(body, nodes, ctrs), out_shape=out_shape,...]
where the time goes in v4:
time: 227 us; the launch traced here: 223 us
  Pallas kernels  211 us (93%)
  local copies, waits for them, and re-layouts  4.75 us (2%)
  other arithmetic  4.65 us (2%)
    pallas_call x4, Pallas kernels, comm_call(): pl.pallas_call(functools.partial(body, nodes, ctrs), out_shape=out_shape,...  107 us
    pallas_call x3, Pallas kernels, apply_kernel(): pl.pallas_call(apply_body, out_shape=jax.ShapeDtypeStruct((owners, width,...  88.1 us
    pallas_call x1, Pallas kernels, node_rows(): pl.pallas_call(node_rows_body, out_shape=[jax.ShapeDtypeStruct((1, 8, cou...  10.4 us

profile of v4, /device:TPU:0, one launch (start us, length us, event | category | flops | bytes accessed | tf_op | source)
XLA Modules:
  0.0 223.3 jit_solution(12897871349515822481)
XLA Ops:
  0.6 0.8 copy.39
  1.4 0.8 copy.38
  2.2 0.7 copy-done.1
  2.9 38.2 %shard_map.68 = (s32[64,128]{1,0:T(8,128)S(1)}, f32[8,8,1024]{2,1,0:T(8,128)S(1)}, f32[4,8,1024]{2,1,0:T(8,128)S(1)}, s32[32,128]{1,0:T(8,128)S(1)}) custom-call(f32[3,16,128]{2,1,0:T(8,128)S(1)} %bitcast.55, s32[8,128]{1,0:T(8,128)S(1)} %bitcast.58, f32[3,32,128]{2,1,0:T(8,128)S(1)} %bitcast.54), custom_call_target="tpu_custom_call" | custom-call | tf_op jit(solution)/shard_map/pallas_call | solution.py:371
  41.3 1.3 fusion.2
  42.9 0.1 reshape.201
  43.0 0.3 fusion.28
  43.6 0.6 slice.43.count
  44.5 10.4 %shard_map.69 = (f32[1,8,4096]{2,1,0:T(8,128)S(1)}, f32[1,12,32,128]{3,2,1,0:T(8,128)S(1)}) custom-call(s32[4096]{0:T(1024)S(1)} %add_select_fusion.3.slab_ref, s32[4096]{0:T(1024)S(1)} %bitcast.57, f32[8,4096]{1,0:T(8,128)S(1)} %maximum_maximum_fusion.xyz_ref, f32[12,4096]{1,0:T(8,128)S(1)} %copy-done), custom_call_target="tpu_custom_call" | custom-call | tf_op jit(solution)/shard_map/pallas_call | solution.py:269
  55.7 0.2 fusion.5
  56.0 0.2 subtract_select_fusion.1
  56.1 1.4 select_reduce_fusion.1
  57.6 2.8 %shard_map.70 = (bf16[8192,128]{1,0:T(8,128)(2,1)S(1)}, bf16[32,128,256]{2,1,0:T(8,128)(2,1)}, bf16[32,128,256]{2,1,0:T(8,128)(2,1)}) custom-call(f32[8,8,1024]{2,1,0:T(8,128)S(1)} %get-tuple-element.18.row_ref, f32[4,8,1024]{2,1,0:T(8,128)S(1)} %get-tuple-element.17.col_ref, f32[1,8,4096]{2,1,0:T(8,128)S(1)} %get-tuple-element.20.node_ref), custom_call_target="tpu_custom_call" | custom-call | tf_op jit(solution)/shard_map/pallas_call | solution.py:220
  60.4 0.6 slice.45.count
  60.9 0.2 subtract_select_fusion
  61.1 1.4 select_reduce_fusion
  62.6 33.0 %shard_map.71.part_ref = f32[8,12,8,128]{3,2,1,0:T(8,128)S(1)} custom-call(s32[1]{0:T(128)} %slice.45.count, s32[2080]{0:T(1024)S(1)} %get-tuple-element.52.items, s32[8448]{0:T(1024)S(1)} %pad.8.order, bf16[8192,128]{1,0:T(8,128)(2,1)S(1)} %get-tuple-element.21.left_ref, bf16[32,128,256]{2,1,0:T(8,128)(2,1)} %get-tuple-element.23.right_ref, ...), custom_call_target="tpu_custom_call" | custom-call | tf_op jit(solution)/shard_map/pallas_call | solution.py:162
  95.6 15.5 %shard_map.72 = (f32[12,8,128]{2,1,0:T(8,128)S(1)}, f32[4,12,8,128]{3,2,1,0:T(8,128)S(1)}) custom-call(f32[8,12,8,128]{3,2,1,0:T(8,128)S(1)} %shard_map.71.part_ref), custom_call_target="tpu_custom_call" | custom-call | tf_op jit(solution)/shard_map/pallas_call | solution.py:371
  111.1 27.5 %shard_map.73.part_ref = f32[8,12,8,128]{3,2,1,0:T(8,128)S(1)} custom-call(s32[1]{0:T(128)} %slice.43.count, s32[2080]{0:T(1024)S(1)} %get-tuple-element.53.items, s32[8448]{0:T(1024)S(1)} %pad.7.order, bf16[8192,128]{1,0:T(8,128)(2,1)S(1)} %get-tuple-element.21.left_ref, bf16[32,128,256]{2,1,0:T(8,128)(2,1)} %get-tuple-element.22.right_ref, ...), custom_call_target="tpu_custom_call" | custom-call | tf_op jit(solution)/shard_map/pallas_call | solution.py:162
  138.6 21.2 %shard_map.74 = (f32[12,8,128]{2,1,0:T(8,128)S(1)}, f32[4,12,8,128]{3,2,1,0:T(8,128)S(1)}, f32[2,12,128]{2,1,0:T(8,128)S(1)}) custom-call(f32[8,12,8,128]{3,2,1,0:T(8,128)S(1)} %shard_map.73.part_ref, f32[12,8,128]{2,1,0:T(8,128)S(1)} %get-tuple-element.26.pulled_ref, f32[4,12,8,128]{3,2,1,0:T(8,128)S(1)} %get-tuple-element.25.vec_ref.pulled_cols), custom_call_target="tpu_custom_call" | custom-call | tf_op jit(solution)/shard_map/pallas_call | solution.py:371
  159.9 27.5 %shard_map.75.part_ref = f32[8,12,8,128]{3,2,1,0:T(8,128)S(1)} custom-call(s32[1]{0:T(128)} %slice.43.count, s32[2080]{0:T(1024)S(1)} %get-tuple-element.53.items, s32[8448]{0:T(1024)S(1)} %pad.7.order, bf16[8192,128]{1,0:T(8,128)(2,1)S(1)} %get-tuple-element.21.left_ref, bf16[32,128,256]{2,1,0:T(8,128)(2,1)} %get-tuple-element.22.right_ref, ...), custom_call_target="tpu_custom_call" | custom-call | tf_op jit(solution)/shard_map/pallas_call | solution.py:162
  187.4 32.5 %shard_map.76.table_ref = f32[8,24,8,128]{3,2,1,0:T(8,128)S(1)} custom-call(f32[8,12,8,128]{3,2,1,0:T(8,128)S(1)} %shard_map.75.part_ref, f32[12,8,128]{2,1,0:T(8,128)S(1)} %get-tuple-element.26.pulled_ref, f32[12,8,128]{2,1,0:T(8,128)S(1)} %get-tuple-element.28.resid_ref, f32[2,12,128]{2,1,0:T(8,128)S(1)} %get-tuple-element.29.scal_ref), custom_call_target="tpu_custom_call" | custom-call | tf_op jit(solution)/shard_map/pallas_call | solution.py:371
  219.9 2.8 %shard_map.77 = f32[24,1024]{1,0:T(8,128)S(1)} custom-call(s32[1024]{0:T(1024)S(1)} %fusion.26.slot_ref, f32[8,24,8,128]{3,2,1,0:T(8,128)S(1)} %shard_map.76.table_ref), custom_call_target="tpu_custom_call" | custom-call | tf_op jit(solution)/shard_map/pallas_call | solution.py:304
  222.7 0.7 fusion.31
  (46 shorter events, 1.8 us)
Async XLA Ops:
  2.2 0.7 copy-start.1
  2.9 41.3 %copy-start.3 = (s32[4096]{0:T(1024)S(1)}, s32[4096]{0:T(1024)}, u32[]{:S(2)}) copy-start(s32[4096]{0:T(1024)} %param.8) | copy-start | bytes 49156
  41.1 3.2 %copy-start.2 = (f32[3,4096]{1,0:T(4,128)S(1)}, f32[3,4096]{1,0:T(4,128)}, u32[]{:S(2)}) copy-start(f32[3,4096]{1,0:T(4,128)} %param.7) | copy-start | bytes 147460
  41.2 3.3 %copy-start = (f32[12,4096]{1,0:T(8,128)S(1)}, f32[12,4096]{1,0:T(8,128)}, u32[]{:S(2)}) copy-start(f32[12,4096]{1,0:T(8,128)} %cot_ref.1) | copy-start | bytes 589828

commit v5 on v4

--- a/solution.py
+++ b/solution.py
@@ -16,6 +16,7 @@
 CELLS = 5
 DEPTH = 64
 PAD = 16
+PIECES = 3
 VMEM = 50 * 1024 * 1024
 NT = (((1,), (1,)), ((), ()))
 MESH = pl.DeviceIdType.MESH
@@ -78,7 +79,7 @@
     start = jnp.sum(jnp.where(passed, batches[:, None], 0), axis=0)
     code = tile * size + (at - start) * BATCH
     items = jnp.where((at < 0) | (tile == total), total * size, code)
-    return ends[-1:], items, jnp.pad((order * GROUP).reshape(-1), (0, size))
+    return jnp.sum(batches, keepdims=True), items, jnp.pad((order * GROUP).reshape(-1), (0, size))
 
 
 def apply_body(count, items, order, left_ref, right_ref, vec_ref, out_ref, acc, vec, q0, q1, k0, k1):
@@ -279,9 +280,10 @@
     )(slab, perm, xyz, cotangent)
 
 
-def pick_body(slot_ref, table_ref, out_ref, rows_a, rows_b):
+def pick_body(slot_ref, table_ref, sol_ref, res_ref, rows_a, rows_b):
     blocks, width, deep, _ = table_ref.shape
-    count = out_ref.shape[1]
+    count = sol_ref.shape[1]
+    half = width // 2
     for block in range(blocks):
         for tile in range(deep):
             rows_a[pl.ds((block * deep + tile) * LANES, LANES), :width] = table_ref[block, :, tile, :].T
@@ -295,7 +297,9 @@
     lax.fori_loop(0, count // 64, gather, 0)
     for tile in range(count // LANES):
         here = pl.ds(tile * LANES, LANES)
-        out_ref[:, here] = rows_b[here, :].T[:width]
+        values = rows_b[here, :].T
+        sol_ref[:, here] = values[:half]
+        res_ref[:, here] = values[half:width]
 
 
 def pick(slots, table):
@@ -303,9 +307,9 @@
     count = slots.shape[0]
     return pl.pallas_call(
         pick_body,
-        out_shape=jax.ShapeDtypeStruct((width, count), jnp.float32),
+        out_shape=[jax.ShapeDtypeStruct((width // 2, count), jnp.float32)] * 2,
         in_specs=[pl.BlockSpec(memory_space=pltpu.SMEM), pl.BlockSpec(memory_space=pltpu.VMEM)],
-        out_specs=pl.BlockSpec(memory_space=pltpu.VMEM),
+        out_specs=[pl.BlockSpec(memory_space=pltpu.VMEM)] * 2,
         scratch_shapes=[
             pltpu.VMEM((blocks * deep * LANES, LANES), jnp.float32),
             pltpu.VMEM((count, LANES), jnp.float32),
@@ -605,11 +609,27 @@
     for v in range(width):
         final[v] = alphas[v] * pulled_ref[v] + seconds[v] * final[v]
         final[width + v] = resid_ref[v] - seconds[v] * final[width + v]
-    copies = [
-        send(final, out_ref.at[links.node], (u0, u1), h - 1, links.on_node(h)) for h in links.node_hops()
-    ]
     out_ref[links.node] = final[...]
-    finish(copies)
+    if nodes % 2:
+        mine = out_ref.at[links.node]
+        finish([send(final, mine, (u0, u1), h - 1, links.on_node(h)) for h in links.node_hops()])
+        return
+    beside = (links.node + 1 - 2 * lax.rem(links.node, 2), links.ctr)
+    half = nodes // 2
+    size = 2 * width // PIECES
+    copies, relays = [], []
+    for piece in range(PIECES):
+        base, rows = piece * (nodes - 1), pl.ds(piece * size, size)
+        mine, target = final.at[rows], out_ref.at[links.node, rows]
+        copies.append([send(mine, target, (u0, u1), base + h, links.on_node(2 * h)) for h in range(1, half)])
+        relays.append(send(mine, target, (u0, u1), base, beside))
+    for piece in range(PIECES):
+        base, rows = piece * (nodes - 1), pl.ds(piece * size, size)
+        for h, copy in zip(range(1, half), copies[piece]):
+            copy.wait()
+            came = out_ref.at[lax.rem(links.node + nodes - 2 * h, nodes), rows]
+            relays.append(send(came, came, (u0, u1), base + half - 1 + h, beside))
+    finish(relays)
 
 
 def local(nodes, ctrs, surface_xyz, centre_idx, volume_xyz, slab_ids, cotangent):
@@ -684,11 +704,10 @@
     final = comm_call(
         second_body, nodes, ctrs, out(nodes, 2 * width, tiles, LANES),
         [landing, vmem(2 * width, tiles, LANES), line, every, scr]
-        + dma_pair(nodes - 1) + dma_pair(devices - 1) + dma_pair(nodes - 1),
+        + dma_pair(nodes - 1) + dma_pair(devices - 1) + dma_pair(PIECES * (nodes - 1)),
         5, part, pulled, resid, scal,
     )
-    final = pick(slots, final)
-    return final[:width], final[width:]
+    return tuple(pick(slots, final))
 
 
 def solution(mesh):

time: 227 us -> 226 us (level); the launches traced: 223 us -> 225 us
  Pallas kernels: 211 us -> 215 us
where the time goes in v5:
time: 226 us; the launch traced here: 225 us
  Pallas kernels  215 us (95%)
  other arithmetic  5.26 us (2%)
  local copies, waits for them, and re-layouts  2.94 us (1%)
    pallas_call x4, Pallas kernels, comm_call(): pl.pallas_call(functools.partial(body, nodes, ctrs), out_shape=out_shape,...  109 us
    pallas_call x3, Pallas kernels, apply_kernel(): pl.pallas_call(apply_body, out_shape=jax.ShapeDtypeStruct((owners, width,...  88.6 us
    pallas_call x1, Pallas kernels, node_rows(): pl.pallas_call(node_rows_body, out_shape=[jax.ShapeDtypeStruct((1, 8, cou...  10.4 us

profile of v5, /device:TPU:0, one launch (start us, length us, event | category | flops | bytes accessed | tf_op | source)
XLA Modules:
  0.0 225.3 jit_solution(16715349608254215513)
XLA Ops:
  0.6 0.8 copy.39
  1.4 0.8 copy.38
  2.3 0.7 copy-done.1
  3.0 38.2 %shard_map.68 = (s32[64,128]{1,0:T(8,128)S(1)}, f32[8,8,1024]{2,1,0:T(8,128)S(1)}, f32[4,8,1024]{2,1,0:T(8,128)S(1)}, s32[32,128]{1,0:T(8,128)S(1)}) custom-call(f32[3,16,128]{2,1,0:T(8,128)S(1)} %bitcast.57, s32[8,128]{1,0:T(8,128)S(1)} %bitcast.60, f32[3,32,128]{2,1,0:T(8,128)S(1)} %bitcast.56), custom_call_target="tpu_custom_call" | custom-call | tf_op jit(solution)/shard_map/pallas_call | solution.py:375
  41.3 1.3 fusion.2
  42.9 10.4 %shard_map.69 = (f32[1,8,4096]{2,1,0:T(8,128)S(1)}, f32[1,12,32,128]{3,2,1,0:T(8,128)S(1)}) custom-call(s32[4096]{0:T(1024)S(1)} %add_select_fusion.3.slab_ref, s32[4096]{0:T(1024)S(1)} %bitcast.59, f32[8,4096]{1,0:T(8,128)S(1)} %maximum_maximum_fusion.xyz_ref, f32[12,4096]{1,0:T(8,128)S(1)} %copy-done), custom_call_target="tpu_custom_call" | custom-call | tf_op jit(solution)/shard_map/pallas_call | solution.py:270
  53.5 0.1 fusion.29
  53.7 0.1 reshape.201
  53.8 0.3 fusion.28
  54.1 0.1 multiply_reduce_fusion
  55.0 0.6 fusion.31
  55.8 0.2 fusion.5
  56.0 0.2 subtract_select_fusion.1
  56.2 1.4 select_reduce_fusion.1
  57.7 2.8 %shard_map.70 = (bf16[8192,128]{1,0:T(8,128)(2,1)S(1)}, bf16[32,128,256]{2,1,0:T(8,128)(2,1)}, bf16[32,128,256]{2,1,0:T(8,128)(2,1)}) custom-call(f32[8,8,1024]{2,1,0:T(8,128)S(1)} %get-tuple-element.18.row_ref, f32[4,8,1024]{2,1,0:T(8,128)S(1)} %get-tuple-element.17.col_ref, f32[1,8,4096]{2,1,0:T(8,128)S(1)} %get-tuple-element.20.node_ref), custom_call_target="tpu_custom_call" | custom-call | tf_op jit(solution)/shard_map/pallas_call | solution.py:221
  60.4 0.2 subtract_select_fusion
  60.6 1.4 select_reduce_fusion
  62.1 33.5 %shard_map.71.part_ref = f32[8,12,8,128]{3,2,1,0:T(8,128)S(1)} custom-call(s32[1]{0:T(128)} %bitcast.10.count, s32[2080]{0:T(1024)S(1)} %add_select_fusion.4.items, s32[8448]{0:T(1024)S(1)} %pad.8.order, bf16[8192,128]{1,0:T(8,128)(2,1)S(1)} %get-tuple-element.21.left_ref, bf16[32,128,256]{2,1,0:T(8,128)(2,1)} %get-tuple-element.23.right_ref, ...), custom_call_target="tpu_custom_call" | custom-call | tf_op jit(solution)/shard_map/pallas_call | solution.py:163
  95.5 15.0 %shard_map.72 = (f32[12,8,128]{2,1,0:T(8,128)S(1)}, f32[4,12,8,128]{3,2,1,0:T(8,128)S(1)}) custom-call(f32[8,12,8,128]{3,2,1,0:T(8,128)S(1)} %shard_map.71.part_ref), custom_call_target="tpu_custom_call" | custom-call | tf_op jit(solution)/shard_map/pallas_call | solution.py:375
  110.6 27.6 %shard_map.73.part_ref = f32[8,12,8,128]{3,2,1,0:T(8,128)S(1)} custom-call(s32[1]{0:T(128)} %bitcast.8.count, s32[2080]{0:T(1024)S(1)} %add_select_fusion.5.items, s32[8448]{0:T(1024)S(1)} %pad.7.order, bf16[8192,128]{1,0:T(8,128)(2,1)S(1)} %get-tuple-element.21.left_ref, bf16[32,128,256]{2,1,0:T(8,128)(2,1)} %get-tuple-element.22.right_ref, ...), custom_call_target="tpu_custom_call" | custom-call | tf_op jit(solution)/shard_map/pallas_call | solution.py:163
  138.2 22.3 %shard_map.74 = (f32[12,8,128]{2,1,0:T(8,128)S(1)}, f32[4,12,8,128]{3,2,1,0:T(8,128)S(1)}, f32[2,12,128]{2,1,0:T(8,128)S(1)}) custom-call(f32[8,12,8,128]{3,2,1,0:T(8,128)S(1)} %shard_map.73.part_ref, f32[12,8,128]{2,1,0:T(8,128)S(1)} %get-tuple-element.26.pulled_ref, f32[4,12,8,128]{3,2,1,0:T(8,128)S(1)} %get-tuple-element.25.vec_ref.pulled_cols), custom_call_target="tpu_custom_call" | custom-call | tf_op jit(solution)/shard_map/pallas_call | solution.py:375
  160.5 27.6 %shard_map.75.part_ref = f32[8,12,8,128]{3,2,1,0:T(8,128)S(1)} custom-call(s32[1]{0:T(128)} %bitcast.8.count, s32[2080]{0:T(1024)S(1)} %add_select_fusion.5.items, s32[8448]{0:T(1024)S(1)} %pad.7.order, bf16[8192,128]{1,0:T(8,128)(2,1)S(1)} %get-tuple-element.21.left_ref, bf16[32,128,256]{2,1,0:T(8,128)(2,1)} %get-tuple-element.22.right_ref, ...), custom_call_target="tpu_custom_call" | custom-call | tf_op jit(solution)/shard_map/pallas_call | solution.py:163
  188.1 33.8 %shard_map.76.table_ref = f32[8,24,8,128]{3,2,1,0:T(8,128)S(1)} custom-call(f32[8,12,8,128]{3,2,1,0:T(8,128)S(1)} %shard_map.75.part_ref, f32[12,8,128]{2,1,0:T(8,128)S(1)} %get-tuple-element.26.pulled_ref, f32[12,8,128]{2,1,0:T(8,128)S(1)} %get-tuple-element.28.resid_ref, f32[2,12,128]{2,1,0:T(8,128)S(1)} %get-tuple-element.29.scal_ref), custom_call_target="tpu_custom_call" | custom-call | tf_op jit(solution)/shard_map/pallas_call | solution.py:375
  221.9 3.5 %shard_map.77 = (f32[12,1024]{1,0:T(8,128)}, f32[12,1024]{1,0:T(8,128)}) custom-call(s32[1024]{0:T(1024)S(1)} %fusion.26.slot_ref, f32[8,24,8,128]{3,2,1,0:T(8,128)S(1)} %shard_map.76.table_ref), custom_call_target="tpu_custom_call" | custom-call | tf_op jit(solution)/shard_map/pallas_call | solution.py:308
  (43 shorter events, 1.5 us)
Async XLA Ops:
  0.6 42.2 %copy-start = (f32[12,4096]{1,0:T(8,128)S(1)}, f32[12,4096]{1,0:T(8,128)}, u32[]{:S(2)}) copy-start(f32[12,4096]{1,0:T(8,128)} %cot_ref.1) | copy-start | bytes 589828
  2.3 0.7 copy-start.1
  3.0 39.6 %copy-start.3 = (s32[4096]{0:T(1024)S(1)}, s32[4096]{0:T(1024)}, u32[]{:S(2)}) copy-start(s32[4096]{0:T(1024)} %param.8) | copy-start | bytes 49156
  3.0 39.7 %copy-start.2 = (f32[3,4096]{1,0:T(4,128)S(1)}, f32[3,4096]{1,0:T(4,128)}, u32[]{:S(2)}) copy-start(f32[3,4096]{1,0:T(4,128)} %param.7) | copy-start | bytes 147460

commit v6 on v5

--- a/solution.py
+++ b/solution.py
@@ -391,20 +391,30 @@
 TN = (((0,), (0,)), ((), ()))
 
 
-def picked(tables, rows, lanes):
-    high = lax.broadcasted_iota(jnp.int32, (tables[0].shape[0], rows.shape[1]), 0) == rows
-    high = jnp.where(high, 1.0, 0.0).astype(jnp.bfloat16)
-    low = lax.broadcasted_iota(jnp.int32, (LANES, rows.shape[1]), 0) == lanes
+def three_parts(tables):
     found = []
     for table in tables:
         a1 = rounded(table)
         a2 = rounded(table - a1)
-        a3 = table - a1 - a2
-        parts = jnp.concatenate([a1, a2, a3], axis=1).astype(jnp.bfloat16)
-        both = lax.dot_general(parts, high, TN, preferred_element_type=jnp.float32)
-        value = both[:LANES] + both[LANES : 2 * LANES] + both[2 * LANES :]
-        found.append(jnp.sum(jnp.where(low, value, 0.0), axis=0, keepdims=True))
+        found += [a1, a2, table - a1 - a2]
+    return jnp.concatenate(found, axis=1).astype(jnp.bfloat16)
+
+
+def picked(parts, rows, lanes):
+    high = lax.broadcasted_iota(jnp.int32, (parts.shape[0], rows.shape[1]), 0) == rows
+    high = jnp.where(high, 1.0, 0.0).astype(jnp.bfloat16)
+    low = lax.broadcasted_iota(jnp.int32, (LANES, rows.shape[1]), 0) == lanes
+    both = lax.dot_general(parts, high, TN, preferred_element_type=jnp.float32)
+    found = []
+    for first in range(0, parts.shape[1], 3 * LANES):
+        one, two, three = (both[first + i * LANES : first + (i + 1) * LANES] for i in range(3))
+        found.append(jnp.sum(jnp.where(low, one + two + three, 0.0), axis=0, keepdims=True))
     return found
+
+
+def spans(tiles):
+    step = 2 - tiles % 2
+    return [range(at, at + step) for at in range(0, tiles, step)]
 
 
 def cell_keys(x, y, z):
@@ -466,13 +476,14 @@
         finish([send(whole, whole, sems[:2], last - 1 + h, links.on_ctr(h)) for h in links.ctr_hops()])
 
     rows, tiles = own_ref.shape[1], mine_ref.shape[1]
-    tables = [all_ref[:, :, k].reshape(-1, LANES) for k in range(3)]
-    for at in range(tiles):
-        ids = ids_ref[at : at + 1, :]
+    parts = three_parts([all_ref[:, :, k].reshape(-1, LANES) for k in range(3)])
+    for span in spans(tiles):
+        ids = jnp.concatenate([ids_ref[at : at + 1, :] for at in span], axis=1)
         device = ids // (rows * LANES)
         place = (device % ctrs * nodes + device // ctrs) * rows + ids // LANES % rows
-        for k, value in enumerate(picked(tables, place, ids % LANES)):
-            mine_ref[k, at : at + 1, :] = value
+        for k, value in enumerate(picked(parts, place, ids % LANES)):
+            for i, at in enumerate(span):
+                mine_ref[k, at : at + 1, :] = value[:, i * LANES : (i + 1) * LANES]
     copies = [
         send(mine_ref, plane_ref.at[links.node], sems[2:4], h - 1, links.on_node(h)) for h in links.node_hops()
     ]
@@ -486,12 +497,14 @@
     count = tables[0].shape[0] * LANES
     keys = sorted_keys(cell_keys(*tables))
     perm_ref[...] = keys.astype(jnp.int32) % count
-    blank = jnp.zeros((4, LANES), jnp.float32)
-    for at in range(tiles):
-        ids = perm_ref[pl.ds(at * nodes + links.node, 1), :]
-        found = [(v - 0.5) * (1.0 / RADIUS) for v in picked(tables, ids // LANES, ids % LANES)]
-        point_ref[:, at * LANES : (at + 1) * LANES] = jnp.concatenate(
-            [blank] + found + [jnp.ones((1, LANES), jnp.float32)], axis=0
+    blank = jnp.zeros((4, 2 * LANES), jnp.float32)
+    parts = three_parts(tables)
+    for span in spans(tiles):
+        ids = jnp.concatenate([perm_ref[pl.ds(at * nodes + links.node, 1), :] for at in span], axis=1)
+        found = [(v - 0.5) * (1.0 / RADIUS) for v in picked(parts, ids // LANES, ids % LANES)]
+        wide = len(span) * LANES
+        point_ref[:, span[0] * LANES : span[0] * LANES + wide] = jnp.concatenate(
+            [blank[:, :wide]] + found + [jnp.ones((1, wide), jnp.float32)], axis=0
         )
     copies = [send(point_ref, node_ref.at[links.node], sems[4:6], h - 1, links.on_node(h)) for h in links.node_hops()]
     copies += [

time: 226 us -> 222 us (0.982)
  Pallas kernels: 215 us -> 211 us
where the time goes in v6:
time: 222 us
  Pallas kernels  211 us (95%)
  other arithmetic  5.26 us (2%)
  local copies, waits for them, and re-layouts  2.94 us (1%)
    pallas_call x4, Pallas kernels, comm_call(): pl.pallas_call(functools.partial(body, nodes, ctrs), out_shape=out_shape,...  108 us
    pallas_call x3, Pallas kernels, apply_kernel(): pl.pallas_call(apply_body, out_shape=jax.ShapeDtypeStruct((owners, width,...  86.8 us
    pallas_call x1, Pallas kernels, node_rows(): pl.pallas_call(node_rows_body, out_shape=[jax.ShapeDtypeStruct((1, 8, cou...  10.4 us

profile of v6, /device:TPU:0, one launch (start us, length us, event | category | flops | bytes accessed | tf_op | source)
XLA Modules:
  0.0 221.8 jit_solution(16051515886554238197)
XLA Ops:
  0.6 0.8 copy.39
  1.4 0.8 copy.38
  2.3 0.7 copy-done.1
  3.0 37.0 %shard_map.68 = (s32[64,128]{1,0:T(8,128)S(1)}, f32[8,8,1024]{2,1,0:T(8,128)S(1)}, f32[4,8,1024]{2,1,0:T(8,128)S(1)}, s32[32,128]{1,0:T(8,128)S(1)}) custom-call(f32[3,16,128]{2,1,0:T(8,128)S(1)} %bitcast.57, s32[8,128]{1,0:T(8,128)S(1)} %bitcast.60, f32[3,32,128]{2,1,0:T(8,128)S(1)} %bitcast.56), custom_call_target="tpu_custom_call" | custom-call | tf_op jit(solution)/shard_map/pallas_call | solution.py:375
  40.2 1.3 fusion.2
  41.7 10.4 %shard_map.69 = (f32[1,8,4096]{2,1,0:T(8,128)S(1)}, f32[1,12,32,128]{3,2,1,0:T(8,128)S(1)}) custom-call(s32[4096]{0:T(1024)S(1)} %add_select_fusion.3.slab_ref, s32[4096]{0:T(1024)S(1)} %bitcast.59, f32[8,4096]{1,0:T(8,128)S(1)} %maximum_maximum_fusion.xyz_ref, f32[12,4096]{1,0:T(8,128)S(1)} %copy-done), custom_call_target="tpu_custom_call" | custom-call | tf_op jit(solution)/shard_map/pallas_call | solution.py:270
  52.3 0.1 fusion.29
  52.5 0.1 reshape.201
  52.7 0.3 fusion.28
  53.0 0.1 multiply_reduce_fusion
  53.8 0.6 fusion.31
  54.6 0.2 fusion.5
  54.9 0.2 subtract_select_fusion.1
  55.0 1.4 select_reduce_fusion.1
  56.5 2.8 %shard_map.70 = (bf16[8192,128]{1,0:T(8,128)(2,1)S(1)}, bf16[32,128,256]{2,1,0:T(8,128)(2,1)}, bf16[32,128,256]{2,1,0:T(8,128)(2,1)}) custom-call(f32[8,8,1024]{2,1,0:T(8,128)S(1)} %get-tuple-element.18.row_ref, f32[4,8,1024]{2,1,0:T(8,128)S(1)} %get-tuple-element.17.col_ref, f32[1,8,4096]{2,1,0:T(8,128)S(1)} %get-tuple-element.20.node_ref), custom_call_target="tpu_custom_call" | custom-call | tf_op jit(solution)/shard_map/pallas_call | solution.py:221
  59.2 0.2 subtract_select_fusion
  59.4 1.4 select_reduce_fusion
  60.9 32.6 %shard_map.71.part_ref = f32[8,12,8,128]{3,2,1,0:T(8,128)S(1)} custom-call(s32[1]{0:T(128)} %bitcast.10.count, s32[2080]{0:T(1024)S(1)} %add_select_fusion.4.items, s32[8448]{0:T(1024)S(1)} %pad.8.order, bf16[8192,128]{1,0:T(8,128)(2,1)S(1)} %get-tuple-element.21.left_ref, bf16[32,128,256]{2,1,0:T(8,128)(2,1)} %get-tuple-element.23.right_ref, ...), custom_call_target="tpu_custom_call" | custom-call | tf_op jit(solution)/shard_map/pallas_call | solution.py:163
  93.4 15.4 %shard_map.72 = (f32[12,8,128]{2,1,0:T(8,128)S(1)}, f32[4,12,8,128]{3,2,1,0:T(8,128)S(1)}) custom-call(f32[8,12,8,128]{3,2,1,0:T(8,128)S(1)} %shard_map.71.part_ref), custom_call_target="tpu_custom_call" | custom-call | tf_op jit(solution)/shard_map/pallas_call | solution.py:375
  108.8 27.1 %shard_map.73.part_ref = f32[8,12,8,128]{3,2,1,0:T(8,128)S(1)} custom-call(s32[1]{0:T(128)} %bitcast.8.count, s32[2080]{0:T(1024)S(1)} %add_select_fusion.5.items, s32[8448]{0:T(1024)S(1)} %pad.7.order, bf16[8192,128]{1,0:T(8,128)(2,1)S(1)} %get-tuple-element.21.left_ref, bf16[32,128,256]{2,1,0:T(8,128)(2,1)} %get-tuple-element.22.right_ref, ...), custom_call_target="tpu_custom_call" | custom-call | tf_op jit(solution)/shard_map/pallas_call | solution.py:163
  135.9 22.3 %shard_map.74 = (f32[12,8,128]{2,1,0:T(8,128)S(1)}, f32[4,12,8,128]{3,2,1,0:T(8,128)S(1)}, f32[2,12,128]{2,1,0:T(8,128)S(1)}) custom-call(f32[8,12,8,128]{3,2,1,0:T(8,128)S(1)} %shard_map.73.part_ref, f32[12,8,128]{2,1,0:T(8,128)S(1)} %get-tuple-element.26.pulled_ref, f32[4,12,8,128]{3,2,1,0:T(8,128)S(1)} %get-tuple-element.25.vec_ref.pulled_cols), custom_call_target="tpu_custom_call" | custom-call | tf_op jit(solution)/shard_map/pallas_call | solution.py:375
  158.2 27.1 %shard_map.75.part_ref = f32[8,12,8,128]{3,2,1,0:T(8,128)S(1)} custom-call(s32[1]{0:T(128)} %bitcast.8.count, s32[2080]{0:T(1024)S(1)} %add_select_fusion.5.items, s32[8448]{0:T(1024)S(1)} %pad.7.order, bf16[8192,128]{1,0:T(8,128)(2,1)S(1)} %get-tuple-element.21.left_ref, bf16[32,128,256]{2,1,0:T(8,128)(2,1)} %get-tuple-element.22.right_ref, ...), custom_call_target="tpu_custom_call" | custom-call | tf_op jit(solution)/shard_map/pallas_call | solution.py:163
  185.4 33.0 %shard_map.76.table_ref = f32[8,24,8,128]{3,2,1,0:T(8,128)S(1)} custom-call(f32[8,12,8,128]{3,2,1,0:T(8,128)S(1)} %shard_map.75.part_ref, f32[12,8,128]{2,1,0:T(8,128)S(1)} %get-tuple-element.26.pulled_ref, f32[12,8,128]{2,1,0:T(8,128)S(1)} %get-tuple-element.28.resid_ref, f32[2,12,128]{2,1,0:T(8,128)S(1)} %get-tuple-element.29.scal_ref), custom_call_target="tpu_custom_call" | custom-call | tf_op jit(solution)/shard_map/pallas_call | solution.py:375
  218.3 3.5 %shard_map.77 = (f32[12,1024]{1,0:T(8,128)}, f32[12,1024]{1,0:T(8,128)}) custom-call(s32[1024]{0:T(1024)S(1)} %fusion.26.slot_ref, f32[8,24,8,128]{3,2,1,0:T(8,128)S(1)} %shard_map.76.table_ref), custom_call_target="tpu_custom_call" | custom-call | tf_op jit(solution)/shard_map/pallas_call | solution.py:308
  (43 shorter events, 1.5 us)
Async XLA Ops:
  0.6 41.1 %copy-start = (f32[12,4096]{1,0:T(8,128)S(1)}, f32[12,4096]{1,0:T(8,128)}, u32[]{:S(2)}) copy-start(f32[12,4096]{1,0:T(8,128)} %cot_ref.1) | copy-start | bytes 589828
  2.3 0.7 copy-start.1
  3.0 38.5 %copy-start.3 = (s32[4096]{0:T(1024)S(1)}, s32[4096]{0:T(1024)}, u32[]{:S(2)}) copy-start(s32[4096]{0:T(1024)} %param.8) | copy-start | bytes 49156
  3.0 38.5 %copy-start.2 = (f32[3,4096]{1,0:T(4,128)S(1)}, f32[3,4096]{1,0:T(4,128)}, u32[]{:S(2)}) copy-start(f32[3,4096]{1,0:T(4,128)} %param.7) | copy-start | bytes 147460

commit v7 on v6

--- a/solution.py
+++ b/solution.py
@@ -258,7 +258,7 @@
 
     lax.fori_loop(0, count // 64, gather, 0)
     for tile in range(count // LANES):
-        here = rows_c[pl.ds(tile * LANES, LANES), :].T
+        here = rows_c[pl.ds(tile * LANES, LANES), : PAD + 8].T
         cot_out[0, :, tile, :] = here[:width]
         xyz_out[0, :, pl.ds(tile * LANES, LANES)] = here[PAD : PAD + 8]
 
@@ -297,7 +297,7 @@
     lax.fori_loop(0, count // 64, gather, 0)
     for tile in range(count // LANES):
         here = pl.ds(tile * LANES, LANES)
-        values = rows_b[here, :].T
+        values = rows_b[here, :width].T
         sol_ref[:, here] = values[:half]
         res_ref[:, here] = values[half:width]
 
@@ -412,6 +412,13 @@
     return found
 
 
+def in_rows(flat, tiled):
+    for at in range(tiled.shape[1]):
+        here = flat[:, at * LANES : (at + 1) * LANES]
+        for k in range(3):
+            tiled[k, at : at + 1, :] = here[k : k + 1]
+
+
 def spans(tiles):
     step = 2 - tiles % 2
     return [range(at, at + step) for at in range(0, tiles, step)]
@@ -451,14 +458,16 @@
 
 
 def setup_body(
-    nodes, ctrs, own_ref, ids_ref, volume_ref, perm_ref, node_ref, ctr_ref, slab_ref,
-    all_ref, mine_ref, plane_ref, table_ref, point_ref, *sems,
+    nodes, ctrs, surface_ref, ids_ref, volume_flat, perm_ref, node_ref, ctr_ref, slab_ref,
+    own_ref, volume_ref, all_ref, mine_ref, plane_ref, table_ref, point_ref, *sems,
 ):
     links = Links(nodes, ctrs)
+    in_rows(surface_ref, own_ref)
     links.meet_sides()
     mine = all_ref.at[links.ctr, links.node]
     copies = [send(own_ref, mine, sems[:2], h - 1, links.on_node(h)) for h in links.node_hops()]
     all_ref[links.ctr, links.node] = own_ref[...]
+    in_rows(volume_flat, volume_ref)
     keys = sorted_keys(cell_keys(*(volume_ref[k] for k in range(3))))
     slab_ref[...] = keys.astype(jnp.int32) % (keys.shape[0] * LANES)
     finish(copies)
@@ -670,18 +679,19 @@
             jax.ShapeDtypeStruct((volume_xyz.shape[1] // LANES, LANES), jnp.int32),
         ),
         [
+            vmem(3, rows, LANES), vmem(3, volume_xyz.shape[1] // LANES, LANES),
             vmem(ctrs, nodes, 3, rows, LANES), vmem(3, tiles, LANES), vmem(nodes, 3, tiles, LANES),
             vmem(3, total // LANES, LANES), vmem(8, owned),
         ] + dma_pair(nodes + ctrs - 2) + dma_pair(nodes - 1) + dma_pair(nodes + ctrs - 2),
-        0, surface_xyz.reshape(3, rows, LANES), centre_idx.reshape(tiles, LANES),
-        volume_xyz.reshape(3, -1, LANES),
+        0, surface_xyz, centre_idx.reshape(tiles, LANES),
+        volume_xyz,
     )
     by_owner = perm.reshape(tiles, nodes, LANES)
     node_points, node_vec = node_rows(slab, node_perm.reshape(-1), volume_points, cotangent)
     left, col_right, node_right = factors(row_points, col_points, node_points)
     flat = lambda value: value.transpose(1, 0, 2).reshape(8, -1)[4:]
     groups = boxes(flat(row_points), GROUP)
-    node_lists = near_lists(boxes(flat(node_points), LANES // 2), groups, 2)
+    node_lists = near_lists(boxes(flat(node_points), LANES // 4), groups, 4)
     col_lists = near_lists(boxes(flat(col_points), LANES), groups, 1)
 
     places = jnp.arange(total, dtype=jnp.int32)

time: 222 us -> 222 us (level)
    pallas_call x4, Pallas kernels: 108 us -> 105 us  [comm_call(): pl.pallas_call(functools.partial(body, nodes, ctrs), out_shape=out_shape,...]
where the time goes in v7:
time: 222 us; the launch traced here: 221 us
  Pallas kernels  210 us (95%)
  other arithmetic  5.37 us (2%)
  local copies, waits for them, and re-layouts  2.89 us (1%)
    pallas_call x4, Pallas kernels, comm_call(): pl.pallas_call(functools.partial(body, nodes, ctrs), out_shape=out_shape,...  105 us
    pallas_call x3, Pallas kernels, apply_kernel(): pl.pallas_call(apply_body, out_shape=jax.ShapeDtypeStruct((owners, width,...  88.5 us
    pallas_call x1, Pallas kernels, node_rows(): pl.pallas_call(node_rows_body, out_shape=[jax.ShapeDtypeStruct((1, 8, cou...  10.4 us

profile of v7, /device:TPU:0, one launch (start us, length us, event | category | flops | bytes accessed | tf_op | source)
XLA Modules:
  0.0 221.2 jit_solution(3339862333671718661)
XLA Ops:
  0.6 0.8 copy-done
  1.5 0.8 copy-done.3
  2.2 0.7 copy-done.4
  2.9 37.0 %shard_map.68 = (s32[64,128]{1,0:T(8,128)S(1)}, f32[8,8,1024]{2,1,0:T(8,128)S(1)}, f32[4,8,1024]{2,1,0:T(8,128)S(1)}, s32[32,128]{1,0:T(8,128)S(1)}) custom-call(f32[3,2048]{1,0:T(4,128)S(1)} %copy-done.3, s32[8,128]{1,0:T(8,128)S(1)} %bitcast.50, f32[3,4096]{1,0:T(4,128)S(1)} %copy-done), custom_call_target="tpu_custom_call" | custom-call | tf_op jit(solution)/shard_map/pallas_call | solution.py:375
  40.2 1.3 fusion.2
  41.7 10.4 %shard_map.69 = (f32[1,8,4096]{2,1,0:T(8,128)S(1)}, f32[1,12,32,128]{3,2,1,0:T(8,128)S(1)}) custom-call(s32[4096]{0:T(1024)S(1)} %add_select_fusion.3.slab_ref, s32[4096]{0:T(1024)S(1)} %bitcast.49, f32[8,4096]{1,0:T(8,128)S(1)} %maximum_maximum_fusion.xyz_ref, f32[12,4096]{1,0:T(8,128)S(1)} %copy-done.2), custom_call_target="tpu_custom_call" | custom-call | tf_op jit(solution)/shard_map/pallas_call | solution.py:270
  52.3 0.2 fusion.29
  52.6 0.1 reshape.193
  52.7 0.3 fusion.28
  53.0 0.2 multiply_reduce_fusion
  53.9 0.6 fusion.31
  54.7 0.2 fusion.5
  54.9 0.2 subtract_select_fusion.1
  55.1 1.4 select_reduce_fusion.1
  56.6 2.8 %shard_map.70 = (bf16[8192,128]{1,0:T(8,128)(2,1)S(1)}, bf16[32,128,256]{2,1,0:T(8,128)(2,1)}, bf16[32,128,256]{2,1,0:T(8,128)(2,1)}) custom-call(f32[8,8,1024]{2,1,0:T(8,128)S(1)} %get-tuple-element.18.row_ref, f32[4,8,1024]{2,1,0:T(8,128)S(1)} %get-tuple-element.17.col_ref, f32[1,8,4096]{2,1,0:T(8,128)S(1)} %get-tuple-element.20.node_ref), custom_call_target="tpu_custom_call" | custom-call | tf_op jit(solution)/shard_map/pallas_call | solution.py:221
  59.3 0.2 subtract_select_fusion
  59.5 1.4 select_reduce_fusion
  61.0 33.4 %shard_map.71.part_ref = f32[8,12,8,128]{3,2,1,0:T(8,128)S(1)} custom-call(s32[1]{0:T(128)} %bitcast.10.count, s32[2080]{0:T(1024)S(1)} %add_select_fusion.4.items, s32[8448]{0:T(1024)S(1)} %pad.8.order, bf16[8192,128]{1,0:T(8,128)(2,1)S(1)} %get-tuple-element.21.left_ref, bf16[32,128,256]{2,1,0:T(8,128)(2,1)} %get-tuple-element.23.right_ref, ...), custom_call_target="tpu_custom_call" | custom-call | tf_op jit(solution)/shard_map/pallas_call | solution.py:163
  94.4 14.4 %shard_map.72 = (f32[12,8,128]{2,1,0:T(8,128)S(1)}, f32[4,12,8,128]{3,2,1,0:T(8,128)S(1)}) custom-call(f32[8,12,8,128]{3,2,1,0:T(8,128)S(1)} %shard_map.71.part_ref), custom_call_target="tpu_custom_call" | custom-call | tf_op jit(solution)/shard_map/pallas_call | solution.py:375
  108.8 27.6 %shard_map.73.part_ref = f32[8,12,8,128]{3,2,1,0:T(8,128)S(1)} custom-call(s32[1]{0:T(128)} %bitcast.8.count, s32[2080]{0:T(1024)S(1)} %add_select_fusion.5.items, s32[8448]{0:T(1024)S(1)} %pad.7.order, bf16[8192,128]{1,0:T(8,128)(2,1)S(1)} %get-tuple-element.21.left_ref, bf16[32,128,256]{2,1,0:T(8,128)(2,1)} %get-tuple-element.22.right_ref, ...), custom_call_target="tpu_custom_call" | custom-call | tf_op jit(solution)/shard_map/pallas_call | solution.py:163
  136.4 22.1 %shard_map.74 = (f32[12,8,128]{2,1,0:T(8,128)S(1)}, f32[4,12,8,128]{3,2,1,0:T(8,128)S(1)}, f32[2,12,128]{2,1,0:T(8,128)S(1)}) custom-call(f32[8,12,8,128]{3,2,1,0:T(8,128)S(1)} %shard_map.73.part_ref, f32[12,8,128]{2,1,0:T(8,128)S(1)} %get-tuple-element.26.pulled_ref, f32[4,12,8,128]{3,2,1,0:T(8,128)S(1)} %get-tuple-element.25.vec_ref.pulled_cols), custom_call_target="tpu_custom_call" | custom-call | tf_op jit(solution)/shard_map/pallas_call | solution.py:375
  158.5 27.6 %shard_map.75.part_ref = f32[8,12,8,128]{3,2,1,0:T(8,128)S(1)} custom-call(s32[1]{0:T(128)} %bitcast.8.count, s32[2080]{0:T(1024)S(1)} %add_select_fusion.5.items, s32[8448]{0:T(1024)S(1)} %pad.7.order, bf16[8192,128]{1,0:T(8,128)(2,1)S(1)} %get-tuple-element.21.left_ref, bf16[32,128,256]{2,1,0:T(8,128)(2,1)} %get-tuple-element.22.right_ref, ...), custom_call_target="tpu_custom_call" | custom-call | tf_op jit(solution)/shard_map/pallas_call | solution.py:163
  186.1 31.6 %shard_map.76.table_ref = f32[8,24,8,128]{3,2,1,0:T(8,128)S(1)} custom-call(f32[8,12,8,128]{3,2,1,0:T(8,128)S(1)} %shard_map.75.part_ref, f32[12,8,128]{2,1,0:T(8,128)S(1)} %get-tuple-element.26.pulled_ref, f32[12,8,128]{2,1,0:T(8,128)S(1)} %get-tuple-element.28.resid_ref, f32[2,12,128]{2,1,0:T(8,128)S(1)} %get-tuple-element.29.scal_ref), custom_call_target="tpu_custom_call" | custom-call | tf_op jit(solution)/shard_map/pallas_call | solution.py:375
  217.7 3.5 %shard_map.77 = (f32[12,1024]{1,0:T(8,128)}, f32[12,1024]{1,0:T(8,128)}) custom-call(s32[1024]{0:T(1024)S(1)} %fusion.26.slot_ref, f32[8,24,8,128]{3,2,1,0:T(8,128)S(1)} %shard_map.76.table_ref), custom_call_target="tpu_custom_call" | custom-call | tf_op jit(solution)/shard_map/pallas_call | solution.py:308
  (45 shorter events, 1.5 us)
Async XLA Ops:
  0.6 0.8 copy-start
  1.5 0.8 copy-start.3
  2.2 0.7 copy-start.4
  2.9 38.5 %copy-start.5 = (s32[4096]{0:T(1024)S(1)}, s32[4096]{0:T(1024)}, u32[]{:S(2)}) copy-start(s32[4096]{0:T(1024)} %param.8) | copy-start | bytes 49156
  2.9 38.5 %copy-start.1 = (f32[3,4096]{1,0:T(4,128)S(1)}, f32[3,4096]{1,0:T(4,128)}, u32[]{:S(2)}) copy-start(f32[3,4096]{1,0:T(4,128)} %volume_flat.1) | copy-start | bytes 147460
  2.9 38.7 %copy-start.2 = (f32[12,4096]{1,0:T(8,128)S(1)}, f32[12,4096]{1,0:T(8,128)}, u32[]{:S(2)}) copy-start(f32[12,4096]{1,0:T(8,128)} %cot_ref.1) | copy-start | bytes 589828
